TPU v7x, 512 devices: a whole 4x8x8 slice. The times are simulated.
512 devices in a mesh: corpus: 128 (over y, z, core), query: 4 (over x).
Axes of the slice: x: 4, y: 8, z: 8, core: 2. Of those that a mesh axis runs over, the one named last changes fastest.
Arguments:
- text_features: bfloat16 [2048, 768], P(('corpus', 'query')), may hold values from -6 to 6
- norm_gain: float32 [768], replicated, may hold values from 0.25 to 1.75
- norm_bias: float32 [768], replicated, may hold values from -3 to 3
- projection: bfloat16 [768, 768], replicated, may hold values from -0.21875 to 0.21875
- image_embeddings: bfloat16 [32768, 768], P('corpus'), may hold values from -6 to 6
- adapter: bfloat16 [768, 768], replicated, may hold values from -0.21875 to 0.21875
- slab_ids: int32 [32768], P('corpus'), may hold values from 0 to 8191
- positive_rows: int32 [2048], P(('corpus', 'query')), may hold values from 0 to 32767
Outputs:
- text_grad: float32 [2048, 768], P(('corpus', 'query'))
- gain_grad: float32 [768], replicated
- bias_grad: float32 [768], replicated
- projection_grad: bfloat16 [768, 768], replicated
- adapter_grad: float32 [768, 768], P('query', 'corpus')
All inputs are finite; a program needn't handle non-finite values.
Results may differ from a plain program's by a relative error of at most 0.015.
Values may be sent and summed in bfloat16 or wider, within the bound.
A program may use at most 64 MiB of HBM per device.

v0:
```python
import jax
import jax.numpy as jnp
from jax import lax
from jax.sharding import PartitionSpec as P

logit_scale = 64.0
epsilon = 1e-05


def forward_queries(text_features, norm_gain, norm_bias, projection):
    features = text_features.astype(jnp.float32)
    average = jnp.mean(features, axis=1, keepdims=True)
    centred = features - average
    spread = jnp.sqrt(jnp.mean(centred * centred, axis=1, keepdims=True) + epsilon)
    normed = centred / spread
    shifted = (normed * norm_gain + norm_bias).astype(jnp.bfloat16)
    raw_query = jnp.dot(shifted, projection, preferred_element_type=jnp.float32)
    length = jnp.sqrt(jnp.sum(raw_query * raw_query, axis=1, keepdims=True) + 1e-06)
    unit_query = raw_query / length
    return (normed, spread, shifted, length, unit_query)


def contract_rows(left, right):
    return lax.dot_general(
        left, right, (((0,), (0,)), ((), ())), preferred_element_type=jnp.float32
    )


def contract_cols(left, right):
    return lax.dot_general(
        left, right, (((1,), (1,)), ((), ())), preferred_element_type=jnp.float32
    )


def shards(
    text_features,
    norm_gain,
    norm_bias,
    projection,
    image_embeddings,
    adapter,
    slab_ids,
    positive_rows,
):
    normed, spread, shifted, length, unit_query = forward_queries(
        text_features, norm_gain, norm_bias, projection
    )
    queries = lax.all_gather(unit_query.astype(jnp.bfloat16), "corpus", axis=0, tiled=True)
    raw_key = jnp.dot(image_embeddings, adapter, preferred_element_type=jnp.float32)
    key_len = jnp.sqrt(jnp.sum(raw_key * raw_key, axis=1, keepdims=True) + 1e-06)
    unit_key = raw_key / key_len
    key_half = unit_key.astype(jnp.bfloat16)
    id_table = lax.all_gather(slab_ids, "corpus", axis=0, tiled=True)
    own_ids = id_table[positive_rows]
    wanted = lax.all_gather(own_ids, "corpus", axis=0, tiled=True)
    matches = slab_ids[None, :] == wanted[:, None]
    first_pass = jnp.exp(logit_scale * contract_cols(queries, key_half))
    totals, pos_totals = lax.psum(
        (
            jnp.sum(first_pass, axis=1),
            jnp.sum(jnp.where(matches, first_pass, jnp.float32(0.0)), axis=1),
        ),
        "corpus",
    )
    weights = (
        logit_scale
        * (
            first_pass / totals[:, None]
            - jnp.where(matches, first_pass / pos_totals[:, None], jnp.float32(0.0))
        )
    ).astype(jnp.bfloat16)
    query_sum = lax.psum_scatter(
        jnp.dot(weights, key_half, preferred_element_type=jnp.float32),
        "corpus",
        scatter_dimension=0,
        tiled=True,
    )
    key_sum = lax.psum(contract_rows(weights, queries).astype(jnp.bfloat16), "query").astype(
        jnp.float32
    )
    key_raw_grad = (
        (key_sum - unit_key * jnp.sum(unit_key * key_sum, axis=1, keepdims=True)) / key_len
    ).astype(jnp.bfloat16)
    model_width = adapter.shape[0]
    row_share = model_width // lax.axis_size("query")
    emb_part = lax.dynamic_slice_in_dim(
        image_embeddings, lax.axis_index("query") * row_share, row_share, 1
    )
    share_grad = contract_rows(emb_part, key_raw_grad)
    adapter_grad = lax.psum_scatter(share_grad, "corpus", scatter_dimension=1, tiled=True)
    query_raw_grad = (
        (query_sum - unit_query * jnp.sum(unit_query * query_sum, axis=1, keepdims=True)) / length
    ).astype(jnp.bfloat16)
    projection_part = contract_rows(shifted, query_raw_grad)
    shifted_grad = contract_cols(query_raw_grad, projection)
    projection_sum, gain_grad, bias_grad = lax.psum(
        (projection_part, jnp.sum(shifted_grad * normed, axis=0), jnp.sum(shifted_grad, axis=0)),
        ("corpus", "query"),
    )
    scaled_grad = shifted_grad * norm_gain
    text_grad = (
        scaled_grad
        - jnp.mean(scaled_grad, axis=1, keepdims=True)
        - normed * jnp.mean(scaled_grad * normed, axis=1, keepdims=True)
    ) / spread
    return (text_grad, gain_grad, bias_grad, projection_sum.astype(jnp.bfloat16), adapter_grad)


def solution(mesh):
    placed = (
        P(("corpus", "query"), None),
        P(),
        P(),
        P(),
        P("corpus", None),
        P(),
        P("corpus"),
        P(("corpus", "query")),
    )
    return jax.shard_map(
        shards,
        mesh=mesh,
        in_specs=placed,
        out_specs=(P(("corpus", "query"), None), P(), P(), P(), P("query", "corpus")),
        check_vma=False,
    )
```

profile of v0, /device:TPU:1, one launch (start us, length us, event | category | flops | bytes accessed | tf_op | source)
XLA Modules:
  0.0 913.6 jit_solution(17793330998575280889)
XLA Ops:
  7.2 0.0 all-reduce.10.cloned.1.call-start
  7.3 0.7 compare_select_fusion.2
  8.0 0.8 convert_reduce_fusion
  8.8 0.9 fusion.17
  9.7 1.4 add_convert_fusion
  11.1 1.7 multiply_reduce_fusion.4
  12.8 58.5 %all-gather.2 = s32[128,1,256]{2,1,0:T(1,128)S(1)} all-gather(s32[1,1,256]{2,1,0:T(1,128)S(1)} %bitcast.17), channel_id=1, replica_groups=mesh['corpus'=128,'query'=4] {'corpus'}, dimensions={0}, use_global_device_ids=true | all-gather | bytes 132096 | tf_op jit(solution)/shard_map/all_gather | solution.py:53
  71.4 0.6 fusion.28
  72.6 0.6 gather_fusion
  73.3 0.2 dynamic-update-slice
  73.5 17.4 %all-reduce = s32[512]{0:T(512)S(1)} all-reduce(s32[512]{0:T(512)S(1)} %dynamic-update-slice), channel_id=2, replica_groups=mesh['corpus'=128,'query'=4] {'corpus'}, use_global_device_ids=true, to_apply=%add | all-reduce | flops 512 | bytes 4096
  90.9 0.1 convert_bitcast_fusion
  91.0 54.0 %all-gather.1 = bf16[128,4,768]{2,1,0:T(4,128)(2,1)S(1)} all-gather(bf16[1,4,768]{2,1,0:T(4,128)(2,1)S(1)} %convert_bitcast_fusion), channel_id=1, replica_groups=mesh['corpus'=128,'query'=4] {'corpus'}, dimensions={0}, use_global_device_ids=true | all-gather | bytes 792576 | tf_op jit(solution)/shard_map/all_gather | solution.py:48
  145.0 0.2 reshape.64
  145.2 0.6 multiply_reduce_fusion
  145.8 1.3 fusion.26
  147.1 246.3 %all-reduce.5 = (f32[512]{0:T(512)S(1)}, f32[512]{0:T(512)S(1)}) all-reduce(f32[512]{0:T(512)S(1)} %get-tuple-element.6, f32[512]{0:T(512)S(1)} %get-tuple-element.5), channel_id=1, replica_groups=mesh['corpus'=128,'query'=4] {'corpus'}, use_global_device_ids=true, to_apply=%region_7.8 | all-reduce | flops 1024 | bytes 8192 | tf_op jit(solution)/shard_map/psum | solution.py:58
  393.4 2.2 convolution_convert_fusion
  395.6 0.0 all-reduce.10.cloned.1.call-update
  395.7 0.0 all-reduce.12.cloned.1.call-start
  395.7 2.7 fusion.11
  398.5 44.3 %all-reduce.10.cloned.1.call-done = bf16[256,768]{1,0:T(8,128)(2,1)} async-done(((bf16[256,768]{1,0:T(8,128)(2,1)}), bf16[256,768]{1,0:T(8,128)(2,1)}) %all-reduce.10.cloned.1.call-update) | async-done | bytes 393232 | tf_op jit(solution)/shard_map/psum | solution.py:78
  442.8 1.3 fusion.2
  444.1 0.5 fusion.9
  444.6 253.5 %fusion = f32[192,8]{0,1:T(8,128)S(1)} fusion(f32[192,768]{0,1:T(8,128)S(1)} %fusion.9), kind=kCustom, calls=%all-reduce-scatter | all-reduce-scatter fusion | flops 196609 | bytes 598016
  698.1 1.3 collective-permute-start.30
  699.4 10.6 %collective-permute-start.31 = (f32[192,6]{0,1:T(8,128)S(1)}, f32[192,6]{0,1:T(8,128)S(1)}, u32[]{:S(2)}, u32[]{:S(2)}) collective-permute-start(f32[192,6]{0,1:T(8,128)S(1)} %slice.2), channel_id=1, source_target_pairs={{0,128},{4,132},{8,136},{12,140},{16,144},{20,148},{24,152},{28,15... | collective-permute-start | bytes 13832
  710.0 1.3 collective-permute-start.29
  711.3 1.3 collective-permute-start.28
  712.6 1.3 collective-permute-start.27
  713.9 1.3 collective-permute-start.26
  715.2 1.3 collective-permute-start.25
  716.5 1.3 collective-permute-start.24
  717.8 1.3 collective-permute-start.23
  719.1 14.0 %collective-permute-start.22 = (f32[192,8]{0,1:T(8,128)S(1)}, f32[192,8]{0,1:T(8,128)S(1)}, u32[]{:S(2)}, u32[]{:S(2)}) collective-permute-start(f32[192,8]{0,1:T(8,128)S(1)} %fusion), channel_id=1, source_target_pairs={{0,92},{4,96},{8,100},{12,104},{16,108},{20,112},{24,116},{28,120}... | collective-permute-start | bytes 18440
  733.1 2.0 collective-permute-start.21
  735.1 1.3 collective-permute-start.20
  736.4 1.3 collective-permute-start.19
  737.7 1.4 collective-permute-start.18
  739.1 1.6 collective-permute-start.17
  740.8 1.9 collective-permute-start.16
  742.7 1.8 collective-permute-start.15
  744.6 2.3 collective-permute-start.14
  746.9 3.7 collective-permute-start.13
  750.6 2.8 collective-permute-start.12
  753.4 2.6 collective-permute-start.11
  756.0 3.1 collective-permute-start.10
  759.1 3.2 collective-permute-start.9
  762.3 4.2 collective-permute-start.8
  766.6 3.4 collective-permute-start.7
  770.0 4.3 collective-permute-start.6
  774.4 3.0 collective-permute-start.5
  777.4 3.4 collective-permute-start.4
  780.9 2.2 collective-permute-start.3
  783.1 4.0 collective-permute-start.2
  787.1 2.5 collective-permute-start.1
  789.6 2.2 collective-permute-start
  793.1 2.9 concatenate
  796.1 0.6 constant_dynamic-slice_fusion
  796.7 0.9 multiply_reduce_fusion.3
  797.6 1.4 fusion.20
  799.1 1.8 multiply_reduce_fusion.1
  800.9 0.7 subtract_divide_fusion
  801.6 105.2 %all-reduce.13 = (f32[768]{0:T(1024)}, f32[768]{0:T(1024)}, bf16[768,768]{1,0:T(8,128)(2,1)}) all-reduce(f32[768]{0:T(1024)S(1)} %get-tuple-element.7, f32[768]{0:T(1024)} %get-tuple-element.10, f32[768,768]{1,0:T(8,128)S(1)} %fusion.20), channel_id=1, replica_groups=mesh['corpus'=128,'query'=4] {'corpus','query'}, use_global_device_ids=true, to_apply=%region_13.14 | all-reduce | flops 591360 | bytes 3551232 | tf_op jit(solution)/shard_map/psum | solution.py:96
  (66 shorter events, 0.2 us)
Async XLA Ops:
  7.2 138.1 %copy-start = (bf16[768,768]{1,0:T(8,128)(2,1)S(1)}, bf16[768,768]{1,0:T(8,128)(2,1)}, u32[]{:S(2)}) copy-start(bf16[768,768]{1,0:T(8,128)(2,1)} %param.13) | copy-start | bytes 3538948
  7.2 64.2 %copy-start.10 = (u32[512]{0:T(512)S(1)}, u32[512]{0:T(512)}, u32[]{:S(2)}) copy-start(u32[512]{0:T(512)} %constant.32) | copy-start | bytes 6148
  7.2 5.6 copy-start.11
  7.2 435.6 %all-reduce.10.cloned.1.call-start = ((), (), s32[]{:S(2)}) async-start(), calls=%async_computation | async-start | bytes 786432 | tf_op jit(solution)/shard_map/psum | solution.py:78
  9.7 1.4 copy-start.8
  11.1 1.7 copy-start.5
  12.8 784.8 %copy-start.7 = (f32[4]{0:T(128)}, f32[4]{0:T(128)S(1)}, u32[]{:S(2)}) copy-start(f32[4]{0:T(128)S(1)} %add_sqrt_fusion.1) | copy-start | bytes 52
  91.0 54.2 %copy-start.3 = (bf16[256,768]{1,0:T(8,128)(2,1)S(1)}, bf16[256,768]{1,0:T(8,128)(2,1)}, u32[]{:S(2)}) copy-start(bf16[256,768]{1,0:T(8,128)(2,1)} %param.12) | copy-start | bytes 1179652
  395.7 401.0 %all-reduce.12.cloned.1.call-start = ((), (), s32[]{:S(2)}) async-start(), calls=%async_computation.1 | async-start | bytes 3145728
  442.8 1.3 copy-start.2
  698.1 17.1 %collective-permute-start.30 = (f32[192,8]{0,1:T(8,128)S(1)}, f32[192,8]{0,1:T(8,128)S(1)}, u32[]{:S(2)}, u32[]{:S(2)}) collective-permute-start(f32[192,8]{0,1:T(8,128)S(1)} %fusion), channel_id=1, source_target_pairs={{0,124},{4,128},{8,132},{12,136},{16,140},{20,144},{24,148},{28,15... | collective-permute-start | bytes 18440
  699.4 14.5 %collective-permute-start.31 = (f32[192,6]{0,1:T(8,128)S(1)}, f32[192,6]{0,1:T(8,128)S(1)}, u32[]{:S(2)}, u32[]{:S(2)}) collective-permute-start(f32[192,6]{0,1:T(8,128)S(1)} %slice.2), channel_id=1, source_target_pairs={{0,128},{4,132},{8,136},{12,140},{16,144},{20,148},{24,152},{28,15... | collective-permute-start | bytes 13832
  710.0 6.5 collective-permute-start.29
  711.3 6.5 collective-permute-start.28
  712.6 6.5 collective-permute-start.27
  713.9 19.2 %collective-permute-start.26 = (f32[192,8]{0,1:T(8,128)S(1)}, f32[192,8]{0,1:T(8,128)S(1)}, u32[]{:S(2)}, u32[]{:S(2)}) collective-permute-start(f32[192,8]{0,1:T(8,128)S(1)} %fusion), channel_id=1, source_target_pairs={{0,108},{4,112},{8,116},{12,120},{16,124},{20,128},{24,132},{28,13... | collective-permute-start | bytes 18440
  715.2 19.9 %collective-permute-start.25 = (f32[192,8]{0,1:T(8,128)S(1)}, f32[192,8]{0,1:T(8,128)S(1)}, u32[]{:S(2)}, u32[]{:S(2)}) collective-permute-start(f32[192,8]{0,1:T(8,128)S(1)} %fusion), channel_id=1, source_target_pairs={{0,104},{4,108},{8,112},{12,116},{16,120},{20,124},{24,128},{28,13... | collective-permute-start | bytes 18440
  716.5 19.9 %collective-permute-start.24 = (f32[192,8]{0,1:T(8,128)S(1)}, f32[192,8]{0,1:T(8,128)S(1)}, u32[]{:S(2)}, u32[]{:S(2)}) collective-permute-start(f32[192,8]{0,1:T(8,128)S(1)} %fusion), channel_id=1, source_target_pairs={{0,100},{4,104},{8,108},{12,112},{16,116},{20,120},{24,124},{28,12... | collective-permute-start | bytes 18440
  717.8 19.9 %collective-permute-start.23 = (f32[192,8]{0,1:T(8,128)S(1)}, f32[192,8]{0,1:T(8,128)S(1)}, u32[]{:S(2)}, u32[]{:S(2)}) collective-permute-start(f32[192,8]{0,1:T(8,128)S(1)} %fusion), channel_id=1, source_target_pairs={{0,96},{4,100},{8,104},{12,108},{16,112},{20,116},{24,120},{28,124... | collective-permute-start | bytes 18440
  719.1 20.0 %collective-permute-start.22 = (f32[192,8]{0,1:T(8,128)S(1)}, f32[192,8]{0,1:T(8,128)S(1)}, u32[]{:S(2)}, u32[]{:S(2)}) collective-permute-start(f32[192,8]{0,1:T(8,128)S(1)} %fusion), channel_id=1, source_target_pairs={{0,92},{4,96},{8,100},{12,104},{16,108},{20,112},{24,116},{28,120}... | collective-permute-start | bytes 18440
  733.1 7.7 collective-permute-start.21
  735.1 7.6 collective-permute-start.20
  736.4 8.2 collective-permute-start.19
  737.7 9.2 %collective-permute-start.18 = (f32[192,8]{0,1:T(8,128)S(1)}, f32[192,8]{0,1:T(8,128)S(1)}, u32[]{:S(2)}, u32[]{:S(2)}) collective-permute-start(f32[192,8]{0,1:T(8,128)S(1)} %fusion), channel_id=1, source_target_pairs={{0,76},{4,80},{8,84},{12,88},{16,92},{20,96},{24,100},{28,104},{32... | collective-permute-start | bytes 18440
  739.1 11.5 %collective-permute-start.17 = (f32[192,8]{0,1:T(8,128)S(1)}, f32[192,8]{0,1:T(8,128)S(1)}, u32[]{:S(2)}, u32[]{:S(2)}) collective-permute-start(f32[192,8]{0,1:T(8,128)S(1)} %fusion), channel_id=1, source_target_pairs={{0,72},{4,76},{8,80},{12,84},{16,88},{20,92},{24,96},{28,100},{32,... | collective-permute-start | bytes 18440
  740.8 12.6 %collective-permute-start.16 = (f32[192,8]{0,1:T(8,128)S(1)}, f32[192,8]{0,1:T(8,128)S(1)}, u32[]{:S(2)}, u32[]{:S(2)}) collective-permute-start(f32[192,8]{0,1:T(8,128)S(1)} %fusion), channel_id=1, source_target_pairs={{0,68},{4,72},{8,76},{12,80},{16,84},{20,88},{24,92},{28,96},{32,1... | collective-permute-start | bytes 18440
  742.7 13.3 %collective-permute-start.15 = (f32[192,8]{0,1:T(8,128)S(1)}, f32[192,8]{0,1:T(8,128)S(1)}, u32[]{:S(2)}, u32[]{:S(2)}) collective-permute-start(f32[192,8]{0,1:T(8,128)S(1)} %fusion), channel_id=1, source_target_pairs={{0,64},{4,68},{8,72},{12,76},{16,80},{20,84},{24,88},{28,92},{32,9... | collective-permute-start | bytes 18440
  744.6 14.5 %collective-permute-start.14 = (f32[192,8]{0,1:T(8,128)S(1)}, f32[192,8]{0,1:T(8,128)S(1)}, u32[]{:S(2)}, u32[]{:S(2)}) collective-permute-start(f32[192,8]{0,1:T(8,128)S(1)} %fusion), channel_id=1, source_target_pairs={{0,60},{4,64},{8,68},{12,72},{16,76},{20,80},{24,84},{28,88},{32,9... | collective-permute-start | bytes 18440
  746.9 15.4 %collective-permute-start.13 = (f32[192,8]{0,1:T(8,128)S(1)}, f32[192,8]{0,1:T(8,128)S(1)}, u32[]{:S(2)}, u32[]{:S(2)}) collective-permute-start(f32[192,8]{0,1:T(8,128)S(1)} %fusion), channel_id=1, source_target_pairs={{0,56},{4,60},{8,64},{12,68},{16,72},{20,76},{24,80},{28,84},{32,8... | collective-permute-start | bytes 18440
  750.6 15.9 %collective-permute-start.12 = (f32[192,8]{0,1:T(8,128)S(1)}, f32[192,8]{0,1:T(8,128)S(1)}, u32[]{:S(2)}, u32[]{:S(2)}) collective-permute-start(f32[192,8]{0,1:T(8,128)S(1)} %fusion), channel_id=1, source_target_pairs={{0,52},{4,56},{8,60},{12,64},{16,68},{20,72},{24,76},{28,80},{32,8... | collective-permute-start | bytes 18440
  753.4 16.6 %collective-permute-start.11 = (f32[192,8]{0,1:T(8,128)S(1)}, f32[192,8]{0,1:T(8,128)S(1)}, u32[]{:S(2)}, u32[]{:S(2)}) collective-permute-start(f32[192,8]{0,1:T(8,128)S(1)} %fusion), channel_id=1, source_target_pairs={{0,48},{4,52},{8,56},{12,60},{16,64},{20,68},{24,72},{28,76},{32,8... | collective-permute-start | bytes 18440
  756.0 18.3 %collective-permute-start.10 = (f32[192,8]{0,1:T(8,128)S(1)}, f32[192,8]{0,1:T(8,128)S(1)}, u32[]{:S(2)}, u32[]{:S(2)}) collective-permute-start(f32[192,8]{0,1:T(8,128)S(1)} %fusion), channel_id=1, source_target_pairs={{0,44},{4,48},{8,52},{12,56},{16,60},{20,64},{24,68},{28,72},{32,7... | collective-permute-start | bytes 18440
  759.1 18.3 %collective-permute-start.9 = (f32[192,8]{0,1:T(8,128)S(1)}, f32[192,8]{0,1:T(8,128)S(1)}, u32[]{:S(2)}, u32[]{:S(2)}) collective-permute-start(f32[192,8]{0,1:T(8,128)S(1)} %fusion), channel_id=1, source_target_pairs={{0,40},{4,44},{8,48},{12,52},{16,56},{20,60},{24,64},{28,68},{32,7... | collective-permute-start | bytes 18440
  762.3 18.5 %collective-permute-start.8 = (f32[192,8]{0,1:T(8,128)S(1)}, f32[192,8]{0,1:T(8,128)S(1)}, u32[]{:S(2)}, u32[]{:S(2)}) collective-permute-start(f32[192,8]{0,1:T(8,128)S(1)} %fusion), channel_id=1, source_target_pairs={{0,36},{4,40},{8,44},{12,48},{16,52},{20,56},{24,60},{28,64},{32,6... | collective-permute-start | bytes 18440
  766.6 16.5 %collective-permute-start.7 = (f32[192,8]{0,1:T(8,128)S(1)}, f32[192,8]{0,1:T(8,128)S(1)}, u32[]{:S(2)}, u32[]{:S(2)}) collective-permute-start(f32[192,8]{0,1:T(8,128)S(1)} %fusion), channel_id=1, source_target_pairs={{0,32},{4,36},{8,40},{12,44},{16,48},{20,52},{24,56},{28,60},{32,6... | collective-permute-start | bytes 18440
  770.0 17.0 %collective-permute-start.6 = (f32[192,8]{0,1:T(8,128)S(1)}, f32[192,8]{0,1:T(8,128)S(1)}, u32[]{:S(2)}, u32[]{:S(2)}) collective-permute-start(f32[192,8]{0,1:T(8,128)S(1)} %fusion), channel_id=1, source_target_pairs={{0,28},{4,32},{8,36},{12,40},{16,44},{20,48},{24,52},{28,56},{32,6... | collective-permute-start | bytes 18440
  774.4 15.2 %collective-permute-start.5 = (f32[192,8]{0,1:T(8,128)S(1)}, f32[192,8]{0,1:T(8,128)S(1)}, u32[]{:S(2)}, u32[]{:S(2)}) collective-permute-start(f32[192,8]{0,1:T(8,128)S(1)} %fusion), channel_id=1, source_target_pairs={{0,24},{4,28},{8,32},{12,36},{16,40},{20,44},{24,48},{28,52},{32,5... | collective-permute-start | bytes 18440
  777.4 15.6 %collective-permute-start.4 = (f32[192,8]{0,1:T(8,128)S(1)}, f32[192,8]{0,1:T(8,128)S(1)}, u32[]{:S(2)}, u32[]{:S(2)}) collective-permute-start(f32[192,8]{0,1:T(8,128)S(1)} %fusion), channel_id=1, source_target_pairs={{0,20},{4,24},{8,28},{12,32},{16,36},{20,40},{24,44},{28,48},{32,5... | collective-permute-start | bytes 18440
  780.9 12.2 %collective-permute-start.3 = (f32[192,8]{0,1:T(8,128)S(1)}, f32[192,8]{0,1:T(8,128)S(1)}, u32[]{:S(2)}, u32[]{:S(2)}) collective-permute-start(f32[192,8]{0,1:T(8,128)S(1)} %fusion), channel_id=1, source_target_pairs={{0,16},{4,20},{8,24},{12,28},{16,32},{20,36},{24,40},{28,44},{32,4... | collective-permute-start | bytes 18440
  783.1 10.0 %collective-permute-start.2 = (f32[192,8]{0,1:T(8,128)S(1)}, f32[192,8]{0,1:T(8,128)S(1)}, u32[]{:S(2)}, u32[]{:S(2)}) collective-permute-start(f32[192,8]{0,1:T(8,128)S(1)} %fusion), channel_id=1, source_target_pairs={{0,12},{4,16},{8,20},{12,24},{16,28},{20,32},{24,36},{28,40},{32,4... | collective-permute-start | bytes 18440
  787.1 6.0 collective-permute-start.1
  789.6 3.5 collective-permute-start
  797.6 1.4 copy-start.1
  797.6 1.4 copy-start.4
  797.6 1.4 copy-start.6
  799.0 1.9 copy-start.9
Sparse Core Ops, SparseCore 0:
  395.8 46.9 all-reduce.9
  446.4 202.0 all-reduce.11
where the time goes:
time: 915 us; the launch traced here: 914 us
  blocking collectives  735 us (80%)
  starting transfers between devices  93.2 us (10%)
  waiting for transfers between devices  44.4 us (5%)
  between operations  16.7 us (2%)
  matrix products  12.2 us (1%)
    unnamed x2, blocking collectives  271 us
    psum x1, blocking collectives, shards(): lax.psum((jnp.sum(first_pass, axis=1), jnp.sum(jnp.where(matches, first_p...  246 us
    psum x1, blocking collectives, shards(): lax.psum((projection_part, jnp.sum(shifted_grad * normed, axis=0), jnp.su...  105 us
    unnamed x33, starting transfers between devices  93.2 us
    all_gather x1, blocking collectives, shards(): id_table = lax.all_gather(slab_ids, 'corpus', axis=0, tiled=True)  58.5 us
    all_gather x1, blocking collectives, shards(): lax.all_gather(unit_query.astype(jnp.bfloat16), 'corpus', axis=0, tiled=T...  54 us
    psum x1, waiting for transfers between devices, shards(): lax.psum(contract_rows(weights, queries).astype(jnp.bfloat16), 'query')  44.3 us
  transfers between devices with their start and end apart: 34, of which 1 were waited for; matrix products, arithmetic and copies ran while one was open for 29% of the time, Pallas kernels for 0%

commit v1 on v0

v1 whole, which is shorter than its diff:
```python
import functools

import jax
import jax.numpy as jnp
from jax import lax
from jax.experimental import pallas as pl
from jax.experimental.pallas import tpu as pltpu
from jax.sharding import PartitionSpec as P

F32 = jnp.float32
BF16 = jnp.bfloat16
MESH = pl.DeviceIdType.MESH

D = 768
SLAB = 256
ROWS = 4
NA = 8
NX = 4
GROUP = 512
ORDER = (1, 7, 2, 6, 3, 5, 4)
XORDER = (1, 3, 2)


def dot(a, b):
    return jnp.dot(a, b, preferred_element_type=F32)


def dot_rows(a, b):
    return lax.dot_general(a, b, (((0,), (0,)), ((), ())), preferred_element_type=F32)


def dot_cols(a, b):
    return lax.dot_general(a, b, (((1,), (1,)), ((), ())), preferred_element_type=F32)


def iota(shape, axis):
    return lax.broadcasted_iota(jnp.int32, shape, axis)


def fold_matrix():
    row, col = iota((128, 128), 0), iota((128, 128), 1)
    source = ((row // 4) % 8) * 16 + 4 * (row // 32) + row % 4
    return jnp.where(source == col, F32(1.0), F32(0.0)).astype(BF16)


def fold_four(rows):
    return jnp.concatenate(
        [rows[:, :256], rows[:, 256:512], rows[:, 512:], jnp.zeros((ROWS, 256), F32)], axis=0
    )


def normalise(features, gain, bias):
    average = jnp.mean(features, axis=1, keepdims=True)
    centred = features - average
    spread = jnp.sqrt(jnp.mean(centred * centred, axis=1, keepdims=True) + 1e-5)
    normed = centred / spread
    return normed, spread, (normed * gain + bias).astype(BF16)


def unit_rows(raw):
    length = jnp.sqrt(jnp.sum(raw * raw, axis=1, keepdims=True) + 1e-6)
    return raw / length, length


def kernel(
    msg_ref, tf_ref, gain_ref, bias_ref, proj_ref, emb_ref, adapter_ref, ids_ref,
    text_out, gb_out, proj_out, adapter_out,
    g1, g2, own_norm, own_unit, own_col, unit_key, key_half, key_len, emb_sel, perm,
    normed_all, shifted_all, query_half, xt, expo, pexpo, weights,
    stat_send, stat_core, stat_a, stat_b,
    q_send, q_own, q_core, qb_send, qb_recv, qa_send, qa_recv, qrg_all,
    k_send, k_recv, krg, s_own, s_send, s_core, sb_send, sb_recv, sa_send, sa_recv, s_wide,
    p_send, p_recv, p_out, gb_recv,
    ag1_ss, ag1_rs, st_ss, st_rs, q_ss, q_rs, ag2_ss, ag2_rs, k_ss, k_rs, s_ss, s_rs, p_ss, p_rs,
    out_sem,
):
    corpus = lax.axis_index("corpus")
    x = lax.axis_index("query")
    c = lax.rem(corpus, 2)
    y = corpus // 16
    z = lax.rem(corpus // 2, 8)
    a = z + c * (y - z)
    b = y + c * (z - y)
    step_a = 2 + 14 * c
    step_b = 16 - 14 * c

    def on_a(k):
        place = lax.rem(a + k, NA)
        return place, (place * step_a + b * step_b + c, x)

    def on_b(k):
        place = lax.rem(b + k, NA)
        return place, (a * step_a + place * step_b + c, x)

    def on_x(k):
        place = lax.rem(x + k, NX)
        return place, (corpus, place)

    partner = (corpus + 1 - 2 * c, x)
    pending = []

    def send(src, dst, send_sem, recv_sem, device):
        copy = pltpu.make_async_remote_copy(
            src_ref=src, dst_ref=dst, send_sem=send_sem, recv_sem=recv_sem,
            device_id=device, device_id_type=MESH,
        )
        copy.start()
        pending.append(copy)

    def arrived(dst, recv_sem):
        pltpu.make_async_remote_copy(
            src_ref=dst, dst_ref=dst, send_sem=recv_sem, recv_sem=recv_sem,
            device_id=partner, device_id_type=MESH,
        ).wait_recv()

    barrier = pltpu.get_barrier_semaphore()
    pl.semaphore_signal(barrier, inc=1, device_id=partner, device_id_type=MESH)
    for k in range(1, NA):
        pl.semaphore_signal(barrier, inc=1, device_id=on_a(k)[1], device_id_type=MESH)
        pl.semaphore_signal(barrier, inc=1, device_id=on_b(k)[1], device_id_type=MESH)
    for k in range(1, NX):
        pl.semaphore_signal(barrier, inc=1, device_id=on_x(k)[1], device_id_type=MESH)

    gain = gain_ref[...]
    bias = bias_ref[...]
    g1[0, b, pl.ds(pl.multiple_of(a * 16, 16), 16), :] = msg_ref[...]
    pl.semaphore_wait(barrier, 2 * (NA - 1) + NX)

    def gather_start(g, ss, rs):
        own = g.at[0, b, pl.ds(pl.multiple_of(a * 16, 16), 16), :]
        for k in ORDER:
            send(own, own, ss.at[k], rs.at[k], on_a(k)[1])

    def gather_middle(g, ss, rs):
        for k in ORDER:
            place = on_a(NA - k)[0]
            arrived(g.at[0, b, pl.ds(pl.multiple_of(place * 16, 16), 16), :], rs.at[k])
        for k in ORDER:
            send(g.at[0, b], g.at[0, b], ss.at[8 + k], rs.at[8 + k], on_b(k)[1])
        send(g.at[0, b], g.at[1, b], ss.at[16], rs.at[16], partner)

    def gather_forward(g, ss, rs):
        for k in ORDER:
            place = on_b(NA - k)[0]
            arrived(g.at[0, place], rs.at[8 + k])
            send(g.at[0, place], g.at[1, place], ss.at[16 + k], rs.at[16 + k], partner)

    def gather_end(g, ss, rs):
        arrived(g.at[1, a], rs.at[16])
        for k in ORDER:
            arrived(g.at[1, lax.rem(a + NA - k, NA)], rs.at[16 + k])

    gather_start(g1, ag1_ss, ag1_rs)

    @pl.loop(0, SLAB // 128)
    def _(i):
        rows = pl.ds(pl.multiple_of(i * 128, 128), 128)
        unit, length = unit_rows(dot(emb_ref[rows, :], adapter_ref[...]))
        unit_key[rows, :] = unit
        key_half[rows, :] = unit.astype(BF16)
        key_len[rows, :] = jnp.broadcast_to(length, (128, 128))

    gather_middle(g1, ag1_ss, ag1_rs)

    pick = jnp.where(
        (iota((D, 256), 0) == iota((D, 256), 1) + x * 192) & (iota((D, 256), 1) < 192),
        F32(1.0), F32(0.0),
    ).astype(BF16)
    emb_sel[...] = dot(emb_ref[...], pick).astype(BF16)

    own4 = tf_ref[...].astype(F32)
    own16 = jnp.concatenate([own4, own4, own4, own4], axis=0)
    normed, spread, shifted = normalise(own16, gain, bias)
    unit, length = unit_rows(dot(shifted, proj_ref[...]))
    own_norm[...] = normed
    own_unit[...] = unit
    own_col[0] = jnp.broadcast_to(spread, (16, 128))
    own_col[1] = jnp.broadcast_to(length, (16, 128))

    gather_forward(g1, ag1_ss, ag1_rs)

    place = iota((1, 1024), 1)
    core = lax.rem(place // 512 + c, 2)
    place_b, place_a = (place // 64) % 8, (place // 8) % 8
    place_y = jnp.where(core == 0, place_b, place_a)
    place_z = place_a + place_b - place_y
    column = jnp.where(
        place % 8 < 6, 6 * (place_y * 16 + place_z * 2 + core) + place % 8, -1
    )

    @pl.loop(0, D // 128)
    def _(i):
        rows = pl.ds(pl.multiple_of(i * 128, 128), 128)
        perm[rows, :] = jnp.where(
            iota((128, 1024), 0) + i * 128 == column, F32(1.0), F32(0.0)
        ).astype(BF16)

    gather_end(g1, ag1_ss, ag1_rs)

    unfold = fold_matrix()

    @pl.loop(0, 4)
    def _(i):
        tables = []
        for j in range(4):
            block = dot(unfold, g1[i // 2, (i % 2) * 4 + j])
            features = jnp.concatenate([block[0:32], block[32:64], block[64:96]], axis=1)
            normed, _, shifted = normalise(features, gain, bias)
            rows = pl.ds(pl.multiple_of(i * 128 + j * 32, 32), 32)
            normed_all[rows, :] = normed
            shifted_all[rows, :] = shifted
            tables.append(block[96:128])
        table = jnp.concatenate(tables, axis=0)
        xt[:, pl.ds(pl.multiple_of(i * 128, 128), 128)] = table.T

    @pl.loop(0, 4)
    def _(i):
        rows = pl.ds(pl.multiple_of(i * 128, 128), 128)
        unit, _ = unit_rows(dot(shifted_all[rows, :], proj_ref[...]))
        query_half[rows, :] = unit.astype(BF16)

    high = xt[128:129, :].astype(jnp.int32)
    low = xt[129:130, :].astype(jnp.int32)
    lane = xt[130:131, :].astype(jnp.int32)
    slot = lax.rem(high * 8 + low + 256 * c, 512)
    choose = jnp.where(iota((512, 512), 0) == slot, F32(1.0), F32(0.0)).astype(BF16)
    found = dot(xt[0:128, :].astype(BF16), choose)
    where_row = iota((128, 512), 0)
    target = jnp.sum(
        jnp.where(where_row == lane, found * 128.0, F32(0.0))
        + jnp.where(where_row == lane + 64, found, F32(0.0)),
        axis=0, keepdims=True,
    )
    own_ids = jnp.broadcast_to(ids_ref[...].astype(F32), (128, SLAB)).T[:, 0:1]

    totals, positives = [], []
    for i in range(4):
        cols = slice(i * 128, i * 128 + 128)
        e = jnp.exp(64.0 * dot_cols(key_half[...], query_half[cols, :]))
        p = jnp.where(own_ids == target[:, cols], e, F32(0.0))
        expo[:, cols] = e
        pexpo[:, cols] = p
        totals.append(jnp.sum(e, axis=0, keepdims=True))
        positives.append(jnp.sum(p, axis=0, keepdims=True))
    mine = jnp.concatenate(totals + positives, axis=0)
    stat_send[0] = jnp.concatenate(
        [totals[2], totals[3], totals[0], totals[1],
         positives[2], positives[3], positives[0], positives[1]], axis=0
    )

    send(stat_send.at[0], stat_core, st_ss.at[0], st_rs.at[0], partner)
    arrived(stat_core, st_rs.at[0])
    mine = mine + stat_core[...]
    stat_a[a] = mine
    for k in ORDER:
        send(stat_a.at[a], stat_a.at[a], st_ss.at[k], st_rs.at[k], on_a(k)[1])
    for k in ORDER:
        arrived(stat_a.at[on_a(NA - k)[0]], st_rs.at[k])
    stat_b[b] = jnp.sum(stat_a[...], axis=0)
    for k in ORDER:
        send(stat_b.at[b], stat_b.at[b], st_ss.at[8 + k], st_rs.at[8 + k], on_b(k)[1])
    for k in ORDER:
        arrived(stat_b.at[on_b(NA - k)[0]], st_rs.at[8 + k])
    factors = 64.0 / jnp.sum(stat_b[...], axis=0)

    for i in (2, 3, 0, 1):
        cols = slice(i * 128, i * 128 + 128)
        weights[:, cols] = (
            expo[:, cols] * factors[i:i + 1, :] - pexpo[:, cols] * factors[4 + i:5 + i, :]
        ).astype(BF16)

    q_send[...] = dot_rows(weights[:, 256:512], key_half[...]).astype(BF16)
    send(q_send, q_core, q_ss.at[0], q_rs.at[0], partner)
    q_own[...] = dot_rows(weights[:, 0:256], key_half[...])

    @pl.loop(0, NX)
    def _(i):
        rows = pl.ds(pl.multiple_of(i * 64, 64), 64)
        k_send[i] = dot(weights[rows, :], query_half[...]).astype(BF16)

    for k in XORDER:
        there, device = on_x(k)
        send(k_send.at[there], k_recv.at[x], k_ss.at[k], k_rs.at[k], device)
    k_recv[x] = k_send[x]

    arrived(q_core, q_rs.at[0])

    @pl.loop(0, NA)
    def _(i):
        rows = pl.ds(pl.multiple_of(i * 32, 32), 32)
        qb_send[i] = (q_own[rows, :] + q_core[rows, :].astype(F32)).astype(BF16)

    for k in ORDER:
        there, device = on_b(k)
        send(qb_send.at[there], qb_recv.at[b], q_ss.at[8 + k], q_rs.at[8 + k], device)
    qb_recv[b] = qb_send[b]

    for k in XORDER:
        arrived(k_recv.at[on_x(NX - k)[0]], k_rs.at[k])
    quarter = pl.ds(pl.multiple_of(x * 64, 64), 64)
    key_sum = (
        (k_recv[0].astype(F32) + k_recv[1].astype(F32)) + k_recv[2].astype(F32)
    ) + k_recv[3].astype(F32)
    unit = unit_key[quarter, :]
    krg[x] = (
        (key_sum - unit * jnp.sum(unit * key_sum, axis=1, keepdims=True))
        / key_len[quarter, 0:1]
    ).astype(BF16)
    for k in XORDER:
        send(krg.at[x], krg.at[x], k_ss.at[4 + k], k_rs.at[4 + k], on_x(k)[1])

    for k in ORDER:
        arrived(qb_recv.at[on_b(NA - k)[0]], q_rs.at[8 + k])
    part = qb_recv[0].astype(F32)
    for i in range(1, NA):
        part = part + qb_recv[i].astype(F32)
    part = part.astype(BF16)
    stacked = jnp.concatenate(
        [part[:, 0:256], part[:, 256:512], part[:, 512:768], jnp.zeros((32, 256), BF16)], axis=0
    )
    folded = dot_rows(unfold, stacked).astype(BF16)
    for i in range(NA):
        qa_send[i] = folded[i * 16:i * 16 + 16, :]
    for k in ORDER:
        there, device = on_a(k)
        send(qa_send.at[there], qa_recv.at[a], q_ss.at[k], q_rs.at[k], device)
    qa_recv[a] = qa_send[a]

    for k in XORDER:
        arrived(krg.at[on_x(NX - k)[0]], k_rs.at[4 + k])
    grads = krg[...].reshape(SLAB, D)

    @pl.loop(0, 4)
    def _(i):
        half = i // 2
        cols = pl.ds(pl.multiple_of((3 - i) * 256, 256), 256)
        spread_out = dot(grads, perm[:, cols]).astype(BF16)
        share = dot_rows(spread_out, emb_sel[...])
        rows = pl.ds(pl.multiple_of((3 - i) * 256, 256), 256)
        s_own[rows, :] = share

    s_send[...] = s_own[512:1024, :].astype(BF16)
    send(s_send, s_core, s_ss.at[0], s_rs.at[0], partner)

    for k in ORDER:
        arrived(qa_recv.at[on_a(NA - k)[0]], q_rs.at[k])
    part = qa_recv[0].astype(F32)
    for i in range(1, NA):
        part = part + qa_recv[i].astype(F32)
    four = jnp.concatenate([part[0:4], part[4:8], part[8:12]], axis=1)
    query_sum = jnp.concatenate([four, four, four, four], axis=0)
    unit = own_unit[...]
    qrg = (
        query_sum - unit * jnp.sum(unit * query_sum, axis=1, keepdims=True)
    ) / own_col[1, :, 0:1]
    g2[0, b, pl.ds(pl.multiple_of(a * 16, 16), 16), :] = fold_four(qrg[0:4]).astype(BF16)
    gather_start(g2, ag2_ss, ag2_rs)

    arrived(s_core, s_rs.at[0])
    for i in range(NA):
        rows = slice(i * 64, i * 64 + 64)
        sb_send[i] = (s_own[rows, :] + s_core[rows, :].astype(F32)).astype(BF16)
    for k in ORDER:
        there, device = on_b(k)
        send(sb_send.at[there], sb_recv.at[b], s_ss.at[8 + k], s_rs.at[8 + k], device)
    sb_recv[b] = sb_send[b]

    gather_middle(g2, ag2_ss, ag2_rs)

    shifted_grad = dot_cols(qrg.astype(BF16), proj_ref[...])
    scaled = shifted_grad * gain
    normed = own_norm[...]
    text = (
        scaled
        - jnp.mean(scaled, axis=1, keepdims=True)
        - normed * jnp.mean(scaled * normed, axis=1, keepdims=True)
    ) / own_col[0, :, 0:1]
    text_out[...] = text[0:4]

    for k in ORDER:
        arrived(sb_recv.at[on_b(NA - k)[0]], s_rs.at[8 + k])
    part = sb_recv[0].astype(F32)
    for i in range(1, NA):
        part = part + sb_recv[i].astype(F32)
    for i in range(NA):
        sa_send[i] = part[i * 8:i * 8 + 8, :]
    for k in ORDER:
        there, device = on_a(k)
        send(sa_send.at[there], sa_recv.at[a], s_ss.at[k], s_rs.at[k], device)
    sa_recv[a] = sa_send[a]

    gather_forward(g2, ag2_ss, ag2_rs)

    for k in ORDER:
        arrived(sa_recv.at[on_a(NA - k)[0]], s_rs.at[k])
    s_wide[...] = jnp.zeros((128, 256), F32)
    s_wide[0:8, :] = jnp.sum(sa_recv[...], axis=0)
    adapter_out[...] = s_wide[...].T[0:192, 0:6]

    gather_end(g2, ag2_ss, ag2_rs)

    @pl.loop(0, 4)
    def _(i):
        for j in range(4):
            block = dot(unfold, g2[i // 2, (i % 2) * 4 + j])
            rows = pl.ds(pl.multiple_of(i * 128 + j * 32, 32), 32)
            qrg_all[rows, :] = jnp.concatenate(
                [block[0:32], block[32:64], block[64:96]], axis=1
            ).astype(BF16)

    cols = pl.ds(pl.multiple_of(c * 384, 128), 384)
    half = qrg_all[:, cols]
    for i in range(D // 128):
        band = slice(i * 128, i * 128 + 128)
        p_send[band, :] = dot_rows(shifted_all[:, band], half).astype(BF16)
    for k in XORDER:
        there, device = on_x(k)
        send(p_send.at[pl.ds(pl.multiple_of(there * 192, 64), 192), :], p_recv.at[x],
             p_ss.at[k], p_rs.at[k], device)
    p_recv[x] = p_send[pl.ds(pl.multiple_of(x * 192, 64), 192), :]

    gain_sum = jnp.zeros((1, D), F32)
    bias_sum = jnp.zeros((1, D), F32)
    for i in range(4):
        rows = slice(i * 128, i * 128 + 128)
        grad = dot_cols(qrg_all[rows, :], proj_ref[...])
        gain_sum = gain_sum + jnp.sum(grad * normed_all[rows, :], axis=0, keepdims=True)
        bias_sum = bias_sum + jnp.sum(grad, axis=0, keepdims=True)
    gb_recv[x] = jnp.concatenate([gain_sum, bias_sum, jnp.zeros((6, D), F32)], axis=0)
    for k in XORDER:
        send(gb_recv.at[x], gb_recv.at[x], p_ss.at[4 + k], p_rs.at[4 + k], on_x(k)[1])

    for k in XORDER:
        arrived(p_recv.at[on_x(NX - k)[0]], p_rs.at[k])
    total = (
        (p_recv[0].astype(F32) + p_recv[1].astype(F32)) + p_recv[2].astype(F32)
    ) + p_recv[3].astype(F32)
    p_out[0, x] = total.astype(BF16)
    for k in XORDER:
        send(p_out.at[0, x], p_out.at[0, x], p_ss.at[8 + k], p_rs.at[8 + k], on_x(k)[1])
    send(p_out.at[0, x], p_out.at[1, x], p_ss.at[12], p_rs.at[12], partner)

    for k in XORDER:
        arrived(gb_recv.at[on_x(NX - k)[0]], p_rs.at[4 + k])
    gb_out[...] = jnp.sum(gb_recv[...], axis=0)

    for k in XORDER:
        there = on_x(NX - k)[0]
        arrived(p_out.at[0, there], p_rs.at[8 + k])
        send(p_out.at[0, there], p_out.at[1, there], p_ss.at[12 + k], p_rs.at[12 + k], partner)
    for i in range(NX):
        proj_out[i * 192:i * 192 + 192, cols] = p_out[0, i]
    arrived(p_out.at[1, x], p_rs.at[12])
    for k in XORDER:
        arrived(p_out.at[1, on_x(NX - k)[0]], p_rs.at[12 + k])
    other = pl.ds(pl.multiple_of((1 - c) * 384, 128), 384)
    for i in range(NX):
        proj_out[i * 192:i * 192 + 192, other] = p_out[1, i]

    for copy in pending:
        copy.wait_send()


def message(text_features, slab_ids, positive_rows):
    fold = text_features.reshape(ROWS, 3, 256).transpose(1, 0, 2).reshape(12, 256)
    ids = slab_ids.reshape(ROWS, 64)
    device, inner = positive_rows // 256, positive_rows % 256
    core, y, z = device % 2, device // 16, (device // 2) % 8
    slot = core * 64 + jnp.where(core == 0, y * 8 + z, z * 8 + y)
    row = slot * 4 + inner // 64
    places = jnp.stack([row // 8, row % 8, inner % 64], axis=1)
    rest = jnp.concatenate(
        [ids // 128, ids % 128, places, jnp.zeros((ROWS, 125), jnp.int32)], axis=1
    ).astype(BF16)
    return jnp.concatenate([fold, rest], axis=0)


def shards(
    text_features, norm_gain, norm_bias, projection, image_embeddings, adapter, slab_ids,
    positive_rows,
):
    whole = pl.BlockSpec(memory_space=pltpu.VMEM)
    dma = pltpu.SemaphoreType.DMA
    text_grad, gain_bias, projection_grad, adapter_grad = pl.pallas_call(
        kernel,
        out_shape=(
            jax.ShapeDtypeStruct((ROWS, D), F32),
            jax.ShapeDtypeStruct((8, D), F32),
            jax.ShapeDtypeStruct((D, D), BF16),
            jax.ShapeDtypeStruct((192, 6), F32),
        ),
        in_specs=[whole] * 8,
        out_specs=(whole,) * 4,
        scratch_shapes=[
            pltpu.VMEM((2, NA, 128, 256), BF16),
            pltpu.VMEM((2, NA, 128, 256), BF16),
            pltpu.VMEM((16, D), F32),
            pltpu.VMEM((16, D), F32),
            pltpu.VMEM((2, 16, 128), F32),
            pltpu.VMEM((SLAB, D), F32),
            pltpu.VMEM((SLAB, D), BF16),
            pltpu.VMEM((SLAB, 128), F32),
            pltpu.VMEM((SLAB, 256), BF16),
            pltpu.VMEM((D, 1024), BF16),
            pltpu.VMEM((GROUP, D), F32),
            pltpu.VMEM((GROUP, D), BF16),
            pltpu.VMEM((GROUP, D), BF16),
            pltpu.VMEM((256, GROUP), F32),
            pltpu.VMEM((SLAB, GROUP), F32),
            pltpu.VMEM((SLAB, GROUP), F32),
            pltpu.VMEM((SLAB, GROUP), BF16),
            pltpu.VMEM((1, 8, 128), F32),
            pltpu.VMEM((8, 128), F32),
            pltpu.VMEM((NA, 8, 128), F32),
            pltpu.VMEM((NA, 8, 128), F32),
            pltpu.VMEM((256, D), BF16),
            pltpu.VMEM((256, D), F32),
            pltpu.VMEM((256, D), BF16),
            pltpu.VMEM((NA, 32, D), BF16),
            pltpu.VMEM((NA, 32, D), BF16),
            pltpu.VMEM((NA, 16, 256), BF16),
            pltpu.VMEM((NA, 16, 256), BF16),
            pltpu.VMEM((GROUP, D), BF16),
            pltpu.VMEM((NX, 64, D), BF16),
            pltpu.VMEM((NX, 64, D), BF16),
            pltpu.VMEM((NX, 64, D), BF16),
            pltpu.VMEM((1024, 256), F32),
            pltpu.VMEM((512, 256), BF16),
            pltpu.VMEM((512, 256), BF16),
            pltpu.VMEM((NA, 64, 256), BF16),
            pltpu.VMEM((NA, 64, 256), BF16),
            pltpu.VMEM((NA, 8, 256), F32),
            pltpu.VMEM((NA, 8, 256), F32),
            pltpu.VMEM((128, 256), F32),
            pltpu.VMEM((D, 384), BF16),
            pltpu.VMEM((NX, 192, 384), BF16),
            pltpu.VMEM((2, NX, 192, 384), BF16),
            pltpu.VMEM((NX, 8, D), F32),
            dma((24,)), dma((24,)),
            dma((16,)), dma((16,)),
            dma((16,)), dma((16,)),
            dma((24,)), dma((24,)),
            dma((8,)), dma((8,)),
            dma((16,)), dma((16,)),
            dma((16,)), dma((16,)),
            dma,
        ],
        compiler_params=pltpu.CompilerParams(
            collective_id=0, has_side_effects=True, vmem_limit_bytes=48 * 1024 * 1024
        ),
    )(
        message(text_features, slab_ids, positive_rows),
        text_features,
        norm_gain.reshape(1, D),
        norm_bias.reshape(1, D),
        projection,
        image_embeddings,
        adapter,
        slab_ids.reshape(1, SLAB),
    )
    return text_grad, gain_bias[0], gain_bias[1], projection_grad, adapter_grad


def solution(mesh):
    placed = (
        P(("corpus", "query"), None),
        P(),
        P(),
        P(),
        P("corpus", None),
        P(),
        P("corpus"),
        P(("corpus", "query")),
    )
    return jax.shard_map(
        shards,
        mesh=mesh,
        in_specs=placed,
        out_specs=(P(("corpus", "query"), None), P(), P(), P(), P("query", "corpus")),
        check_vma=False,
    )
```

time: 915 us -> 115 us (0.13)
  blocking collectives: 735 us -> 0 us
  Pallas kernels: 0 us -> 101 us
  starting transfers between devices: 93.2 us -> 0 us
  waiting for transfers between devices: 44.4 us -> 0 us
  between operations: 16.7 us -> 0.66 us
  matrix products: 12.2 us -> 0 us
    psum x2 -> x0, blocking collectives: 351 us -> none  [the longest x1 246 us: shards(): lax.psum((jnp.sum(first_pass, axis=1), jnp.sum(jnp.where(matches, first_p...]
    unnamed x2 -> x0, blocking collectives: 271 us -> none
    all_gather x2 -> x0, blocking collectives: 113 us -> none  [the longest x1 58.5 us: shards(): id_table = lax.all_gather(slab_ids, 'corpus', axis=0, tiled=True)]
    pallas_call x0 -> x1, Pallas kernels: none -> 101 us  [shards(): pl.pallas_call(kernel, out_shape=(jax.ShapeDtypeStruct((ROWS, D), F32), j...]
    unnamed x33 -> x0, starting transfers between devices: 93.2 us -> none
    psum x1 -> x0, waiting for transfers between devices: 44.3 us -> none  [shards(): lax.psum(contract_rows(weights, queries).astype(jnp.bfloat16), 'query')]
    dot_general x8 -> x0, matrix products: 12.2 us -> none  [the longest x3 4.09 us: contract_rows(): lax.dot_general(left, right, (((0,), (0,)), ((), ())), preferred_element_...]
  transfers between devices with their start and end apart: 34 -> 0, of which waited for: 1 -> 0; matrix products, arithmetic and copies ran while one was open for 29% -> 0% of each run, Pallas kernels for 0% -> 0%
where the time goes in v1:
time: 115 us; the launch traced here: 114 us
  Pallas kernels  101 us (88%)
  local copies, waits for them, and re-layouts  11.1 us (10%)
  other arithmetic  1.41 us (1%)
    pallas_call x1, Pallas kernels, shards(): pl.pallas_call(kernel, out_shape=(jax.ShapeDtypeStruct((ROWS, D), F32), j...  101 us
    unnamed x13, local copies, waits for them, and re-layouts  7.19 us

profile of v1, /device:TPU:1, one launch (start us, length us, event | category | flops | bytes accessed | tf_op | source)
XLA Modules:
  0.0 114.2 jit_solution(1891070654697390937)
XLA Ops:
  0.6 0.7 fusion.7
  1.3 0.1 copy.20
  1.4 0.7 fusion.5
  2.1 0.1 copy.19
  2.2 0.1 copy.18
  2.3 0.8 reshape.30
  3.1 0.1 concatenate.7
  3.2 0.7 reshape.31.gain_ref
  3.9 0.7 reshape.32.bias_ref
  4.6 0.7 reshape.29
  5.3 0.0 copy-start
  5.3 1.3 %copy-done = bf16[768,768]{1,0:T(8,128)(2,1)S(1)} copy-done((bf16[768,768]{1,0:T(8,128)(2,1)S(1)}, bf16[768,768]{1,0:T(8,128)(2,1)}, u32[]{:S(2)}) %copy-start) | copy-done | bytes 1179672
  6.6 0.0 copy-start.1
  6.6 1.3 %copy-done.1 = bf16[768,768]{1,0:T(8,128)(2,1)S(1)} copy-done((bf16[768,768]{1,0:T(8,128)(2,1)S(1)}, bf16[768,768]{1,0:T(8,128)(2,1)}, u32[]{:S(2)}) %copy-start.1) | copy-done | bytes 1179672
  7.9 0.0 copy-start.2
  7.9 1.0 copy-done.2
  8.9 0.0 copy-start.3
  8.9 0.7 copy-done.3
  9.5 0.0 copy-start.4
  9.5 0.7 copy-done.4
  10.2 101.1 %shard_map.119 = (f32[4,768]{1,0:T(4,128)S(1)}, f32[8,768]{1,0:T(8,128)S(1)}, bf16[768,768]{1,0:T(8,128)(2,1)S(1)}, f32[192,6]{1,0:T(8,128)S(1)}) custom-call(bf16[16,256]{1,0:T(8,128)(2,1)S(1)} %pad_maximum_fusion.msg_ref, bf16[4,768]{1,0:T(4,128)(2,1)S(1)} %copy-done.3, f32[1,768]{1,0:T(1,128)S(1)} %reshape.31.gain_ref, f32[1,768]{1,0:T(1,128)S(1)} %reshape.32.bias_ref, ...), custom_call_target="tpu_custom_call" | custom-call | tf_op jit(solution)/shard_map/pallas_call | solution.py:484
  111.3 0.7 copy.21
  112.0 0.6 slice_reduce_fusion
  112.6 0.6 copy.24
  113.2 1.0 copy.25
  (4 shorter events, 0.0 us)
Async XLA Ops:
  5.3 1.3 %copy-start = (bf16[768,768]{1,0:T(8,128)(2,1)S(1)}, bf16[768,768]{1,0:T(8,128)(2,1)}, u32[]{:S(2)}) copy-start(bf16[768,768]{1,0:T(8,128)(2,1)} %proj_ref.1) | copy-start | bytes 3538948
  6.6 1.3 %copy-start.1 = (bf16[768,768]{1,0:T(8,128)(2,1)S(1)}, bf16[768,768]{1,0:T(8,128)(2,1)}, u32[]{:S(2)}) copy-start(bf16[768,768]{1,0:T(8,128)(2,1)} %adapter_ref.1) | copy-start | bytes 3538948
  7.9 1.0 copy-start.2
  8.9 0.7 copy-start.3
  9.5 0.7 copy-start.4

commit v2 on v1

v2 whole, which is shorter than its diff:
```python
import functools

import jax
import jax.numpy as jnp
from jax import lax
from jax.experimental import pallas as pl
from jax.experimental.pallas import tpu as pltpu
from jax.sharding import PartitionSpec as P

F32 = jnp.float32
BF16 = jnp.bfloat16
MESH = pl.DeviceIdType.MESH

D = 768
SLAB = 256
ROWS = 4
NA = 8
NX = 4
GROUP = 512
ORDER = (1, 7, 2, 6, 3, 5, 4)
XORDER = (1, 3, 2)


def dot(a, b):
    return jnp.dot(a, b, preferred_element_type=F32)


def dot_rows(a, b):
    return lax.dot_general(a, b, (((0,), (0,)), ((), ())), preferred_element_type=F32)


def dot_cols(a, b):
    return lax.dot_general(a, b, (((1,), (1,)), ((), ())), preferred_element_type=F32)


def iota(shape, axis):
    return lax.broadcasted_iota(jnp.int32, shape, axis)


def fold_matrix():
    row, col = iota((128, 128), 0), iota((128, 128), 1)
    source = ((row // 4) % 8) * 16 + 4 * (row // 32) + row % 4
    return jnp.where(source == col, F32(1.0), F32(0.0)).astype(BF16)


def normalise(features, gain, bias):
    average = jnp.mean(features, axis=1, keepdims=True)
    centred = features - average
    spread = jnp.sqrt(jnp.mean(centred * centred, axis=1, keepdims=True) + 1e-5)
    normed = centred / spread
    return normed, spread, (normed * gain + bias).astype(BF16)


def unit_rows(raw):
    length = jnp.sqrt(jnp.sum(raw * raw, axis=1, keepdims=True) + 1e-6)
    return raw / length, length


def kernel(
    tf_hbm, gain_hbm, bias_hbm, proj_hbm, emb_hbm, adapter_hbm, ids_hbm, rows_hbm,
    text_out, gb_out, proj_out, adapter_out,
    tf_ref, gain_ref, bias_ref, proj_ref, emb_ref, adapter_ref, ids_ref, rows_ref,
    g0, g1, g2, unit_key, key_half, key_len, emb_sel, perm,
    normed_all, shifted_all, query_half, unit_all, len_all, spread_all, xt,
    negs, poss, negs_half, poss_half, weights,
    stat_send, stat_core, stat_a, stat_b,
    q_send, q_own, q_core, qb_send, qb_recv, qa_recv,
    k_send, k_recv, krg, s_own, s_send, s_core, sb_send, sb_recv, sa_send, sa_recv, s_wide,
    p_send, p_recv, p_out, gb_recv,
    ag1_ss, ag1_rs, x_ss, x_rs, st_ss, st_rs, q_ss, q_rs, ag2_ss, ag2_rs, k_ss, k_rs,
    s_ss, s_rs, p_ss, p_rs, in_sem,
):
    corpus = lax.axis_index("corpus")
    x = lax.axis_index("query")
    c = lax.rem(corpus, 2)
    y = corpus // 16
    z = lax.rem(corpus // 2, 8)
    a = z + c * (y - z)
    b = y + c * (z - y)
    step_a = 2 + 14 * c
    step_b = 16 - 14 * c

    def on_a(k):
        place = lax.rem(a + k, NA)
        return place, (place * step_a + b * step_b + c, x)

    def on_b(k):
        place = lax.rem(b + k, NA)
        return place, (a * step_a + place * step_b + c, x)

    def on_x(k):
        place = lax.rem(x + k, NX)
        return place, (corpus, place)

    partner = (corpus + 1 - 2 * c, x)
    pending = []

    def send(src, dst, send_sem, recv_sem, device):
        copy = pltpu.make_async_remote_copy(
            src_ref=src, dst_ref=dst, send_sem=send_sem, recv_sem=recv_sem,
            device_id=device, device_id_type=MESH,
        )
        copy.start()
        pending.append(copy)

    def arrived(dst, recv_sem):
        pltpu.make_async_remote_copy(
            src_ref=dst, dst_ref=dst, send_sem=recv_sem, recv_sem=recv_sem,
            device_id=partner, device_id_type=MESH,
        ).wait_recv()

    barrier = pltpu.get_barrier_semaphore()
    pl.semaphore_signal(barrier, inc=1, device_id=partner, device_id_type=MESH)
    for k in range(1, NA):
        pl.semaphore_signal(barrier, inc=1, device_id=on_a(k)[1], device_id_type=MESH)
        pl.semaphore_signal(barrier, inc=1, device_id=on_b(k)[1], device_id_type=MESH)
    for k in range(1, NX):
        pl.semaphore_signal(barrier, inc=1, device_id=on_x(k)[1], device_id_type=MESH)

    loads = [
        pltpu.make_async_copy(src, dst, in_sem.at[i])
        for i, (src, dst) in enumerate((
            (tf_hbm, tf_ref), (ids_hbm, ids_ref), (rows_hbm, rows_ref), (emb_hbm, emb_ref),
            (adapter_hbm, adapter_ref), (gain_hbm, gain_ref), (bias_hbm, bias_ref),
            (proj_hbm, proj_ref),
        ))
    ]
    for load in loads:
        load.start()

    for load in loads[:3]:
        load.wait()
    id_row = ids_ref[...].reshape(1, SLAB)
    own4 = tf_ref[...].astype(F32)
    row16, col16 = iota((16, SLAB), 0), iota((16, SLAB), 1)
    quarter_ids = jnp.where(col16 // 64 == row16, id_row, 0)
    both = jnp.concatenate([quarter_ids // 128, quarter_ids % 128], axis=1)
    bring = jnp.where(
        iota((512, 128), 1) == iota((512, 128), 0) % 64 + 64 * (iota((512, 128), 0) // 256),
        F32(1.0), F32(0.0),
    ).astype(BF16)
    listed = dot(both.astype(F32).astype(BF16), bring)
    wanted_row = jnp.sum(
        jnp.where(
            iota((16, ROWS), 0) == iota((16, ROWS), 1),
            rows_ref[...].reshape(1, ROWS).astype(F32), F32(0.0),
        ),
        axis=1, keepdims=True,
    ).astype(jnp.int32)
    device, inner = wanted_row // 256, wanted_row % 256
    core, there_y, there_z = device % 2, device // 16, (device // 2) % 8
    slot = core * 64 + jnp.where(core == 0, there_y * 8 + there_z, there_z * 8 + there_y)
    row = slot * 4 + inner // 64
    lane = iota((16, 128), 1)
    places = jnp.where(
        lane == 0, row // 8, jnp.where(lane == 1, row % 8, jnp.where(lane == 2, inner % 64, 0))
    ).astype(F32)
    rest = jnp.concatenate([listed, places], axis=1)
    message = jnp.concatenate(
        [own4[:, :256], own4[:, 256:512], own4[:, 512:], rest[0:4]], axis=0
    ).astype(BF16)
    g0[pl.ds(pl.multiple_of(a * 16, 16), 16), :] = message
    pl.semaphore_wait(barrier, 2 * (NA - 1) + NX)

    own = g0.at[pl.ds(pl.multiple_of(a * 16, 16), 16), :]
    for k in ORDER:
        send(own, own, ag1_ss.at[k], ag1_rs.at[k], on_a(k)[1])

    for load in loads[3:]:
        load.wait()
    gain = gain_ref[...].reshape(1, D)
    bias = bias_ref[...].reshape(1, D)

    @pl.loop(0, SLAB // 128)
    def _(i):
        rows = pl.ds(pl.multiple_of(i * 128, 128), 128)
        unit, length = unit_rows(dot(emb_ref[rows, :], adapter_ref[...]))
        unit_key[rows, :] = unit
        key_half[rows, :] = unit.astype(BF16)
        key_len[rows, :] = jnp.broadcast_to(length, (128, 128))

    for k in ORDER:
        place = on_a(NA - k)[0]
        arrived(g0.at[pl.ds(pl.multiple_of(place * 16, 16), 16), :], ag1_rs.at[k])

    unfold = fold_matrix()
    g1[0, b] = dot(unfold, g0[...]).astype(BF16)
    text_of = lambda region, place: g1.at[region, place, pl.ds(0, 96), :]
    ids_of = lambda region, place: g1.at[region, place, pl.ds(96, 32), :]
    for part, ss, rs in ((text_of, ag1_ss, ag1_rs), (ids_of, x_ss, x_rs)):
        for k in ORDER:
            send(part(0, b), part(0, b), ss.at[8 + k], rs.at[8 + k], on_b(k)[1])
        send(part(0, b), part(1, b), ss.at[16], rs.at[16], partner)

    def forward(part, ss, rs, k):
        place = on_b(NA - k)[0]
        arrived(part(0, place), rs.at[8 + k])
        send(part(0, place), part(1, place), ss.at[16 + k], rs.at[16 + k], partner)

    def from_core(k):
        return lax.rem(a + NA - k, NA) if k else a

    def query_block(region, places):
        shifts = []
        for place in places:
            block = g1[region, place, 0:96, :].astype(F32)
            features = jnp.concatenate([block[0:32], block[32:64], block[64:96]], axis=1)
            normed, spread, shifted = normalise(features, gain, bias)
            rows = pl.ds(pl.multiple_of(region * 256 + place * 32, 32), 32)
            normed_all[rows, :] = normed
            shifted_all[rows, :] = shifted
            if region == 0:
                spread_all[rows, :] = jnp.broadcast_to(spread, (32, 128))
            shifts.append(shifted)
        unit, length = unit_rows(dot(jnp.concatenate(shifts, axis=0), proj_ref[...]))
        for i, place in enumerate(places):
            rows = pl.ds(pl.multiple_of(region * 256 + place * 32, 32), 32)
            piece = slice(i * 32, i * 32 + 32)
            query_half[rows, :] = unit[piece].astype(BF16)
            if region == 0:
                unit_all[rows, :] = unit[piece]
                len_all[rows, :] = jnp.broadcast_to(length[piece], (32, 128))

    near, far = ORDER[:3], ORDER[3:]
    for k in near:
        forward(text_of, ag1_ss, ag1_rs, k)
    query_block(0, [b] + [on_b(NA - k)[0] for k in near])
    for k in (0,) + near:
        arrived(text_of(1, from_core(k)), ag1_rs.at[16 + k])
    query_block(1, [from_core(k) for k in (0,) + near])
    for k in far:
        forward(text_of, ag1_ss, ag1_rs, k)
    query_block(0, [on_b(NA - k)[0] for k in far])
    for k in ORDER:
        forward(ids_of, x_ss, x_rs, k)
    for k in far:
        arrived(text_of(1, from_core(k)), ag1_rs.at[16 + k])
    query_block(1, [from_core(k) for k in far])
    for k in (0,) + ORDER:
        arrived(ids_of(1, from_core(k)), x_rs.at[16 + k])

    for region in range(2):
        for i in range(2):
            table = jnp.concatenate(
                [g1[region, i * 4 + j, 96:128, :] for j in range(4)], axis=0
            ).astype(F32)
            first = region * 256 + i * 128
            xt[:, first:first + 128] = table.T

    high = xt[128:129, :].astype(jnp.int32)
    low = xt[129:130, :].astype(jnp.int32)
    lane = xt[130:131, :].astype(jnp.int32)
    slot = lax.rem(high * 8 + low + 256 * c, 512)
    choose = jnp.where(iota((512, 512), 0) == slot, F32(1.0), F32(0.0)).astype(BF16)
    found = dot(xt[0:128, :].astype(BF16), choose)
    where_row = iota((128, 512), 0)
    target = jnp.sum(
        jnp.where(where_row == lane, found * 128.0, F32(0.0))
        + jnp.where(where_row == lane + 64, found, F32(0.0)),
        axis=0, keepdims=True,
    )
    own_ids = jnp.broadcast_to(id_row.astype(F32), (128, SLAB)).T[:, 0:1]

    negatives, positives = [], []
    for i in range(4):
        cols = slice(i * 128, i * 128 + 128)
        e = jnp.exp(64.0 * dot_cols(key_half[...], query_half[cols, :]))
        hit = own_ids == target[:, cols]
        n = jnp.where(hit, F32(0.0), e)
        p = jnp.where(hit, e, F32(0.0))
        negs[:, cols] = n
        poss[:, cols] = p
        negs_half[:, cols] = n.astype(BF16)
        poss_half[:, cols] = p.astype(BF16)
        negatives.append(jnp.sum(n, axis=0, keepdims=True))
        positives.append(jnp.sum(p, axis=0, keepdims=True))
    mine = jnp.concatenate(negatives + positives, axis=0)
    stat_send[0] = jnp.concatenate(
        [negatives[2], negatives[3], negatives[0], negatives[1],
         positives[2], positives[3], positives[0], positives[1]], axis=0
    )

    send(stat_send.at[0], stat_core, st_ss.at[0], st_rs.at[0], partner)
    for part, half in enumerate((negs_half, poss_half)):
        q_send[part] = dot_rows(half[:, 256:512], key_half[...]).astype(BF16)
        send(q_send.at[part], q_core.at[part], q_ss.at[part], q_rs.at[part], partner)

    arrived(stat_core, st_rs.at[0])
    mine = mine + stat_core[...]
    stat_a[a] = mine
    for k in ORDER:
        send(stat_a.at[a], stat_a.at[a], st_ss.at[k], st_rs.at[k], on_a(k)[1])

    for part, half in enumerate((negs_half, poss_half)):
        q_own[part] = dot_rows(half[:, 0:256], key_half[...])
    for part in range(2):
        arrived(q_core.at[part], q_rs.at[part])

    @pl.loop(0, NA)
    def _(i):
        rows = pl.ds(pl.multiple_of(i * 32, 32), 32)
        for part in range(2):
            qb_send[i, part] = (
                q_own[part, rows, :] + q_core[part, rows, :].astype(F32)
            ).astype(BF16)

    for k in ORDER:
        there, device = on_b(k)
        send(qb_send.at[there], qb_recv.at[b], q_ss.at[8 + k], q_rs.at[8 + k], device)
    qb_recv[b] = qb_send[b]

    for k in ORDER:
        arrived(stat_a.at[on_a(NA - k)[0]], st_rs.at[k])
    stat_b[b] = jnp.sum(stat_a[...], axis=0)
    for k in ORDER:
        send(stat_b.at[b], stat_b.at[b], st_ss.at[8 + k], st_rs.at[8 + k], on_b(k)[1])

    pick = jnp.where(
        (iota((D, 256), 0) == iota((D, 256), 1) + x * 192) & (iota((D, 256), 1) < 192),
        F32(1.0), F32(0.0),
    ).astype(BF16)
    emb_sel[...] = dot(emb_ref[...], pick).astype(BF16)
    place = iota((1, 1024), 1)
    core = lax.rem(place // 512 + c, 2)
    place_b, place_a = (place // 64) % 8, (place // 8) % 8
    place_y = jnp.where(core == 0, place_b, place_a)
    place_z = place_a + place_b - place_y
    column = jnp.where(
        place % 8 < 6, 6 * (place_y * 16 + place_z * 2 + core) + place % 8, -1
    )

    @pl.loop(0, D // 128)
    def _(i):
        rows = pl.ds(pl.multiple_of(i * 128, 128), 128)
        perm[rows, :] = jnp.where(
            iota((128, 1024), 0) + i * 128 == column, F32(1.0), F32(0.0)
        ).astype(BF16)

    for k in ORDER:
        arrived(stat_b.at[on_b(NA - k)[0]], st_rs.at[8 + k])
    stats = jnp.sum(stat_b[...], axis=0)
    by_total = 64.0 / (stats[0:4] + stats[4:8])
    by_positive = 1.0 / stats[4:8]
    share_negative = stats[0:4] * by_total

    for i in range(4):
        cols = slice(i * 128, i * 128 + 128)
        weights[:, cols] = (
            negs[:, cols] * by_total[i:i + 1, :]
            - (poss[:, cols] * by_positive[i:i + 1, :]) * share_negative[i:i + 1, :]
        ).astype(BF16)

    @pl.loop(0, NX)
    def _(i):
        rows = pl.ds(pl.multiple_of(i * 64, 64), 64)
        k_send[i] = dot(weights[rows, :], query_half[...]).astype(BF16)

    for k in XORDER:
        there, device = on_x(k)
        send(k_send.at[there], k_recv.at[x], k_ss.at[k], k_rs.at[k], device)
    k_recv[x] = k_send[x]

    diagonal = iota((32, SLAB), 1) == iota((32, SLAB), 0) + b * 32

    def as_column(rows):
        wide = jnp.concatenate([rows[0:1], rows[1:2]], axis=1)
        return jnp.sum(jnp.where(diagonal, wide, F32(0.0)), axis=1, keepdims=True)

    for k in ORDER:
        arrived(qb_recv.at[on_b(NA - k)[0]], q_rs.at[8 + k])
    sums = []
    for part in range(2):
        total = qb_recv[0, part].astype(F32)
        for i in range(1, NA):
            total = total + qb_recv[i, part].astype(F32)
        sums.append(total)
    qa_recv[a] = (
        sums[0] * as_column(by_total)
        - (sums[1] * as_column(by_positive)) * as_column(share_negative)
    ).astype(BF16)
    for k in ORDER:
        send(qa_recv.at[a], qa_recv.at[a], q_ss.at[16 + k], q_rs.at[16 + k], on_a(k)[1])

    for k in XORDER:
        arrived(k_recv.at[on_x(NX - k)[0]], k_rs.at[k])
    quarter = pl.ds(pl.multiple_of(x * 64, 64), 64)
    key_sum = (
        (k_recv[0].astype(F32) + k_recv[1].astype(F32)) + k_recv[2].astype(F32)
    ) + k_recv[3].astype(F32)
    unit = unit_key[quarter, :]
    krg[x] = (
        (key_sum - unit * jnp.sum(unit * key_sum, axis=1, keepdims=True))
        / key_len[quarter, 0:1]
    ).astype(BF16)
    for k in XORDER:
        send(krg.at[x], krg.at[x], k_ss.at[4 + k], k_rs.at[4 + k], on_x(k)[1])

    for k in XORDER:
        arrived(krg.at[on_x(NX - k)[0]], k_rs.at[4 + k])
    grads = krg[...].reshape(SLAB, D)

    @pl.loop(0, 4)
    def _(i):
        half = i // 2
        cols = pl.ds(pl.multiple_of((3 - i) * 256, 256), 256)
        spread_out = dot(grads, perm[:, cols]).astype(BF16)
        share = dot_rows(spread_out, emb_sel[...])
        rows = pl.ds(pl.multiple_of((3 - i) * 256, 256), 256)
        s_own[rows, :] = share

    s_send[...] = s_own[512:1024, :].astype(BF16)
    send(s_send, s_core, s_ss.at[0], s_rs.at[0], partner)

    for k in ORDER:
        arrived(qa_recv.at[on_a(NA - k)[0]], q_rs.at[16 + k])
    query_sum = qa_recv[0].astype(F32)
    for i in range(1, NA):
        query_sum = query_sum + qa_recv[i].astype(F32)
    block = pl.ds(pl.multiple_of(b * 32, 32), 32)
    unit = unit_all[block, :]
    qrg = (
        (query_sum - unit * jnp.sum(unit * query_sum, axis=1, keepdims=True))
        / len_all[block, 0:1]
    ).astype(BF16)
    g2[0, b] = qrg
    for k in ORDER:
        send(g2.at[0, b], g2.at[0, b], ag2_ss.at[k], ag2_rs.at[k], on_b(k)[1])
    send(g2.at[0, b], g2.at[1, b], ag2_ss.at[8], ag2_rs.at[8], partner)

    arrived(s_core, s_rs.at[0])
    for i in range(NA):
        rows = slice(i * 64, i * 64 + 64)
        sb_send[i] = (s_own[rows, :] + s_core[rows, :].astype(F32)).astype(BF16)
    for k in ORDER:
        there, device = on_b(k)
        send(sb_send.at[there], sb_recv.at[b], s_ss.at[8 + k], s_rs.at[8 + k], device)
    sb_recv[b] = sb_send[b]

    shifted_grad = dot_cols(qrg, proj_ref[...])
    scaled = shifted_grad * gain
    normed = normed_all[block, :]
    text = (
        scaled
        - jnp.mean(scaled, axis=1, keepdims=True)
        - normed * jnp.mean(scaled * normed, axis=1, keepdims=True)
    ) / spread_all[block, 0:1]
    own_text = text[0:4]
    for i in range(1, NA):
        own_text = jnp.where(a == i, text[i * 4:i * 4 + 4], own_text)
    text_out[...] = own_text

    for k in ORDER:
        arrived(sb_recv.at[on_b(NA - k)[0]], s_rs.at[8 + k])
    part = sb_recv[0].astype(F32)
    for i in range(1, NA):
        part = part + sb_recv[i].astype(F32)
    for i in range(NA):
        sa_send[i] = part[i * 8:i * 8 + 8, :]
    for k in ORDER:
        there, device = on_a(k)
        send(sa_send.at[there], sa_recv.at[a], s_ss.at[k], s_rs.at[k], device)
    sa_recv[a] = sa_send[a]

    for k in ORDER:
        place = on_b(NA - k)[0]
        arrived(g2.at[0, place], ag2_rs.at[k])
        send(g2.at[0, place], g2.at[1, place], ag2_ss.at[8 + k], ag2_rs.at[8 + k], partner)

    for k in ORDER:
        arrived(sa_recv.at[on_a(NA - k)[0]], s_rs.at[k])
    s_wide[...] = jnp.zeros((128, 256), F32)
    s_wide[0:8, :] = jnp.sum(sa_recv[...], axis=0)
    adapter_out[...] = s_wide[...].T[0:192, 0:6]

    for k in (0,) + ORDER:
        arrived(g2.at[1, from_core(k)], ag2_rs.at[8 + k])

    cols = pl.ds(pl.multiple_of(c * 384, 128), 384)
    half = g2[:, :, :, cols].reshape(GROUP, 384)
    for i in range(D // 128):
        band = slice(i * 128, i * 128 + 128)
        p_send[band, :] = dot_rows(shifted_all[:, band], half).astype(BF16)
    for h in range(2):
        for k in XORDER:
            there, device = on_x(k)
            send(p_send.at[pl.ds(pl.multiple_of(there * 192 + h * 96, 32), 96), :],
                 p_recv.at[h, x], p_ss.at[4 * h + k], p_rs.at[4 * h + k], device)
        p_recv[h, x] = p_send[pl.ds(pl.multiple_of(x * 192 + h * 96, 32), 96), :]

    gain_sum = jnp.zeros((1, D), F32)
    bias_sum = jnp.zeros((1, D), F32)
    for i in range(4):
        rows = slice(i * 128, i * 128 + 128)
        quads = slice(i % 2 * 4, i % 2 * 4 + 4)
        grad = dot_cols(g2[i // 2, quads].reshape(128, D), proj_ref[...])
        gain_sum = gain_sum + jnp.sum(grad * normed_all[rows, :], axis=0, keepdims=True)
        bias_sum = bias_sum + jnp.sum(grad, axis=0, keepdims=True)
    gb_recv[x] = jnp.concatenate([gain_sum, bias_sum, jnp.zeros((6, D), F32)], axis=0)
    for k in XORDER:
        send(gb_recv.at[x], gb_recv.at[x], p_ss.at[8 + k], p_rs.at[8 + k], on_x(k)[1])

    for h in range(2):
        for k in XORDER:
            arrived(p_recv.at[h, on_x(NX - k)[0]], p_rs.at[4 * h + k])
        total = (
            (p_recv[h, 0].astype(F32) + p_recv[h, 1].astype(F32)) + p_recv[h, 2].astype(F32)
        ) + p_recv[h, 3].astype(F32)
        p_out[0, x, h] = total.astype(BF16)
        for k in XORDER:
            send(p_out.at[0, x, h], p_out.at[0, x, h],
                 p_ss.at[12 + 4 * h + k], p_rs.at[12 + 4 * h + k], on_x(k)[1])
        send(p_out.at[0, x, h], p_out.at[1, x, h], p_ss.at[20 + 4 * h], p_rs.at[20 + 4 * h], partner)

    for k in XORDER:
        arrived(gb_recv.at[on_x(NX - k)[0]], p_rs.at[8 + k])
    gb_out[...] = jnp.sum(gb_recv[...], axis=0)

    for h in range(2):
        for k in XORDER:
            there = on_x(NX - k)[0]
            arrived(p_out.at[0, there, h], p_rs.at[12 + 4 * h + k])
            send(p_out.at[0, there, h], p_out.at[1, there, h],
                 p_ss.at[20 + 4 * h + k], p_rs.at[20 + 4 * h + k], partner)
    for i in range(NX):
        proj_out[i * 192:i * 192 + 192, cols] = p_out[0, i].reshape(192, 384)
    other = pl.ds(pl.multiple_of((1 - c) * 384, 128), 384)
    for h in range(2):
        arrived(p_out.at[1, x, h], p_rs.at[20 + 4 * h])
        for k in XORDER:
            arrived(p_out.at[1, on_x(NX - k)[0], h], p_rs.at[20 + 4 * h + k])
    for i in range(NX):
        proj_out[i * 192:i * 192 + 192, other] = p_out[1, i].reshape(192, 384)

    for copy in pending:
        copy.wait_send()


def shards(
    text_features, norm_gain, norm_bias, projection, image_embeddings, adapter, slab_ids,
    positive_rows,
):
    whole = pl.BlockSpec(memory_space=pltpu.VMEM)
    dma = pltpu.SemaphoreType.DMA
    text_grad, gain_bias, projection_grad, adapter_grad = pl.pallas_call(
        kernel,
        out_shape=(
            jax.ShapeDtypeStruct((ROWS, D), F32),
            jax.ShapeDtypeStruct((8, D), F32),
            jax.ShapeDtypeStruct((D, D), BF16),
            jax.ShapeDtypeStruct((192, 6), F32),
        ),
        in_specs=[pl.BlockSpec(memory_space=pl.ANY)] * 8,
        out_specs=(whole,) * 4,
        scratch_shapes=[
            pltpu.VMEM((ROWS, D), BF16),
            pltpu.VMEM((D,), F32),
            pltpu.VMEM((D,), F32),
            pltpu.VMEM((D, D), BF16),
            pltpu.VMEM((SLAB, D), BF16),
            pltpu.VMEM((D, D), BF16),
            pltpu.VMEM((SLAB,), jnp.int32),
            pltpu.VMEM((ROWS,), jnp.int32),
            pltpu.VMEM((128, 256), BF16),
            pltpu.VMEM((2, NA, 128, 256), BF16),
            pltpu.VMEM((2, NA, 32, D), BF16),
            pltpu.VMEM((SLAB, D), F32),
            pltpu.VMEM((SLAB, D), BF16),
            pltpu.VMEM((SLAB, 128), F32),
            pltpu.VMEM((SLAB, 256), BF16),
            pltpu.VMEM((D, 1024), BF16),
            pltpu.VMEM((GROUP, D), F32),
            pltpu.VMEM((GROUP, D), BF16),
            pltpu.VMEM((GROUP, D), BF16),
            pltpu.VMEM((GROUP // 2, D), F32),
            pltpu.VMEM((GROUP // 2, 128), F32),
            pltpu.VMEM((GROUP // 2, 128), F32),
            pltpu.VMEM((256, GROUP), F32),
            pltpu.VMEM((SLAB, GROUP), F32),
            pltpu.VMEM((SLAB, GROUP), F32),
            pltpu.VMEM((SLAB, GROUP), BF16),
            pltpu.VMEM((SLAB, GROUP), BF16),
            pltpu.VMEM((SLAB, GROUP), BF16),
            pltpu.VMEM((1, 8, 128), F32),
            pltpu.VMEM((8, 128), F32),
            pltpu.VMEM((NA, 8, 128), F32),
            pltpu.VMEM((NA, 8, 128), F32),
            pltpu.VMEM((2, 256, D), BF16),
            pltpu.VMEM((2, 256, D), F32),
            pltpu.VMEM((2, 256, D), BF16),
            pltpu.VMEM((NA, 2, 32, D), BF16),
            pltpu.VMEM((NA, 2, 32, D), BF16),
            pltpu.VMEM((NA, 32, D), BF16),
            pltpu.VMEM((NX, 64, D), BF16),
            pltpu.VMEM((NX, 64, D), BF16),
            pltpu.VMEM((NX, 64, D), BF16),
            pltpu.VMEM((1024, 256), F32),
            pltpu.VMEM((512, 256), BF16),
            pltpu.VMEM((512, 256), BF16),
            pltpu.VMEM((NA, 64, 256), BF16),
            pltpu.VMEM((NA, 64, 256), BF16),
            pltpu.VMEM((NA, 8, 256), F32),
            pltpu.VMEM((NA, 8, 256), F32),
            pltpu.VMEM((128, 256), F32),
            pltpu.VMEM((D, 384), BF16),
            pltpu.VMEM((2, NX, 96, 384), BF16),
            pltpu.VMEM((2, NX, 2, 96, 384), BF16),
            pltpu.VMEM((NX, 8, D), F32),
            dma((24,)), dma((24,)),
            dma((24,)), dma((24,)),
            dma((16,)), dma((16,)),
            dma((24,)), dma((24,)),
            dma((16,)), dma((16,)),
            dma((8,)), dma((8,)),
            dma((16,)), dma((16,)),
            dma((28,)), dma((28,)),
            dma((8,)),
        ],
        compiler_params=pltpu.CompilerParams(
            collective_id=0, has_side_effects=True, vmem_limit_bytes=48 * 1024 * 1024
        ),
    )(
        text_features,
        norm_gain,
        norm_bias,
        projection,
        image_embeddings,
        adapter,
        slab_ids,
        positive_rows,
    )
    return text_grad, gain_bias[0], gain_bias[1], projection_grad, adapter_grad


def solution(mesh):
    placed = (
        P(("corpus", "query"), None),
        P(),
        P(),
        P(),
        P("corpus", None),
        P(),
        P("corpus"),
        P(("corpus", "query")),
    )
    return jax.shard_map(
        shards,
        mesh=mesh,
        in_specs=placed,
        out_specs=(P(("corpus", "query"), None), P(), P(), P(), P("query", "corpus")),
        check_vma=False,
    )
```

time: 115 us -> 110 us (0.957)
  Pallas kernels: 101 us -> 99.5 us
  other arithmetic: 1.41 us -> 0 us
  local copies, waits for them, and re-layouts: 11.1 us -> 9.83 us
    reshape x4 -> x0, local copies, waits for them, and re-layouts: 2.84 us -> none  [the longest x1 0.76 us: message(): ids = slab_ids.reshape(ROWS, 64)]
    unnamed x13 -> x19, local copies, waits for them, and re-layouts: 7.19 us -> 9.22 us
    pallas_call x1, Pallas kernels: 101 us -> 99.5 us  [shards(): pl.pallas_call(kernel, out_shape=(jax.ShapeDtypeStruct((ROWS, D), F32), j...]
    another operation x4 -> x0, other arithmetic: 1.39 us -> none  [the longest x3 1.38 us: message(): places = jnp.stack([row // 8, row % 8, inner % 64], axis=1)]
where the time goes in v2:
time: 110 us
  Pallas kernels  99.5 us (90%)
  local copies, waits for them, and re-layouts  9.83 us (9%)
    pallas_call x1, Pallas kernels, shards(): pl.pallas_call(kernel, out_shape=(jax.ShapeDtypeStruct((ROWS, D), F32), j...  99.5 us
    unnamed x19, local copies, waits for them, and re-layouts  9.22 us

profile of v2, /device:TPU:1, one launch (start us, length us, event | category | flops | bytes accessed | tf_op | source)
XLA Modules:
  0.0 110.0 jit_solution(5068899100035137050)
XLA Ops:
  0.6 0.0 copy-start
  0.6 1.3 %copy-done = bf16[768,768]{1,0:T(8,128)(2,1)S(1)} copy-done((bf16[768,768]{1,0:T(8,128)(2,1)S(1)}, bf16[768,768]{1,0:T(8,128)(2,1)}, u32[]{:S(2)}) %copy-start) | copy-done | bytes 1179672
  1.9 0.0 copy-start.1
  1.9 1.3 %copy-done.1 = bf16[768,768]{1,0:T(8,128)(2,1)S(1)} copy-done((bf16[768,768]{1,0:T(8,128)(2,1)S(1)}, bf16[768,768]{1,0:T(8,128)(2,1)}, u32[]{:S(2)}) %copy-start.1) | copy-done | bytes 1179672
  3.2 0.0 copy-start.2
  3.2 1.0 copy-done.2
  4.2 0.0 copy-start.3
  4.2 0.7 copy-done.3
  4.9 0.0 copy-start.4
  4.9 0.7 copy-done.4
  5.6 0.0 copy-start.5
  5.6 0.7 copy-done.5
  6.2 0.0 copy-start.6
  6.2 0.7 copy-done.6
  6.9 0.0 copy-start.7
  6.9 0.7 copy-done.7
  7.6 99.5 %shard_map.119 = (f32[4,768]{1,0:T(4,128)S(1)}, f32[8,768]{1,0:T(8,128)S(1)}, bf16[768,768]{1,0:T(8,128)(2,1)S(1)}, f32[192,6]{1,0:T(8,128)S(1)}) custom-call(bf16[4,768]{1,0:T(4,128)(2,1)S(1)} %copy-done.3, f32[768]{0:T(1024)S(1)} %copy-done.4, f32[768]{0:T(1024)S(1)} %copy-done.5, bf16[768,768]{1,0:T(8,128)(2,1)S(1)} %copy-done, ...), custom_call_target="tpu_custom_call" | custom-call | tf_op jit(solution)/shard_map/pallas_call | solution.py:544
  107.1 0.7 copy.13
  107.8 0.6 slice_reduce_fusion
  108.4 0.6 copy.16
  109.0 1.0 copy.17
Async XLA Ops:
  0.6 1.3 %copy-start = (bf16[768,768]{1,0:T(8,128)(2,1)S(1)}, bf16[768,768]{1,0:T(8,128)(2,1)}, u32[]{:S(2)}) copy-start(bf16[768,768]{1,0:T(8,128)(2,1)} %proj_hbm.1) | copy-start | bytes 3538948
  1.9 1.3 %copy-start.1 = (bf16[768,768]{1,0:T(8,128)(2,1)S(1)}, bf16[768,768]{1,0:T(8,128)(2,1)}, u32[]{:S(2)}) copy-start(bf16[768,768]{1,0:T(8,128)(2,1)} %adapter_hbm.1) | copy-start | bytes 3538948
  3.2 1.0 copy-start.2
  4.2 0.7 copy-start.3
  4.9 0.7 copy-start.4
  5.6 0.7 copy-start.5
  6.2 0.7 copy-start.6
  6.9 0.7 copy-start.7

commit v3 on v2

--- a/solution.py
+++ b/solution.py
@@ -37,35 +37,34 @@
     return lax.broadcasted_iota(jnp.int32, shape, axis)
 
 
-def fold_matrix():
-    row, col = iota((128, 128), 0), iota((128, 128), 1)
-    source = ((row // 4) % 8) * 16 + 4 * (row // 32) + row % 4
-    return jnp.where(source == col, F32(1.0), F32(0.0)).astype(BF16)
+def spread_matrix():
+    row, col = iota((32, 128), 0), iota((32, 128), 1)
+    return jnp.where((row >> 2) * 16 + (row & 3) == col, F32(1.0), F32(0.0)).astype(BF16)
 
 
 def normalise(features, gain, bias):
     average = jnp.mean(features, axis=1, keepdims=True)
     centred = features - average
     spread = jnp.sqrt(jnp.mean(centred * centred, axis=1, keepdims=True) + 1e-5)
-    normed = centred / spread
+    normed = centred * (1.0 / spread)
     return normed, spread, (normed * gain + bias).astype(BF16)
 
 
 def unit_rows(raw):
     length = jnp.sqrt(jnp.sum(raw * raw, axis=1, keepdims=True) + 1e-6)
-    return raw / length, length
+    return raw * (1.0 / length), length
 
 
 def kernel(
     tf_hbm, gain_hbm, bias_hbm, proj_hbm, emb_hbm, adapter_hbm, ids_hbm, rows_hbm,
-    text_out, gb_out, proj_out, adapter_out,
+    small_out, proj_out,
     tf_ref, gain_ref, bias_ref, proj_ref, emb_ref, adapter_ref, ids_ref, rows_ref,
-    g0, g1, g2, unit_key, key_half, key_len, emb_sel, perm,
+    gt, g0, g1, gx, g2, unit_key, key_half, key_len, emb_sel, perm,
     normed_all, shifted_all, query_half, unit_all, len_all, spread_all, xt,
     negs, poss, negs_half, poss_half, weights,
     stat_send, stat_core, stat_a, stat_b,
     q_send, q_own, q_core, qb_send, qb_recv, qa_recv,
-    k_send, k_recv, krg, s_own, s_send, s_core, sb_send, sb_recv, sa_send, sa_recv, s_wide,
+    k_send, k_recv, krg, s_own, s_send, s_core, sb_send, sb_recv, sa_send, sa_recv,
     p_send, p_recv, p_out, gb_recv,
     ag1_ss, ag1_rs, x_ss, x_rs, st_ss, st_rs, q_ss, q_rs, ag2_ss, ag2_rs, k_ss, k_rs,
     s_ss, s_rs, p_ss, p_rs, in_sem,
@@ -128,15 +127,20 @@
     for load in loads:
         load.start()
 
-    for load in loads[:3]:
+    loads[0].wait()
+    gt[a] = tf_ref[...]
+    pl.semaphore_wait(barrier, 2 * (NA - 1) + NX)
+    for k in ORDER:
+        send(gt.at[a], gt.at[a], ag1_ss.at[k], ag1_rs.at[k], on_a(k)[1])
+
+    for load in loads[1:3]:
         load.wait()
     id_row = ids_ref[...].reshape(1, SLAB)
-    own4 = tf_ref[...].astype(F32)
     row16, col16 = iota((16, SLAB), 0), iota((16, SLAB), 1)
-    quarter_ids = jnp.where(col16 // 64 == row16, id_row, 0)
-    both = jnp.concatenate([quarter_ids // 128, quarter_ids % 128], axis=1)
+    quarter_ids = jnp.where(col16 >> 6 == row16, id_row, 0)
+    both = jnp.concatenate([quarter_ids >> 7, quarter_ids & 127], axis=1)
     bring = jnp.where(
-        iota((512, 128), 1) == iota((512, 128), 0) % 64 + 64 * (iota((512, 128), 0) // 256),
+        iota((512, 128), 1) == (iota((512, 128), 0) & 63) + 64 * (iota((512, 128), 0) >> 8),
         F32(1.0), F32(0.0),
     ).astype(BF16)
     listed = dot(both.astype(F32).astype(BF16), bring)
@@ -147,24 +151,19 @@
         ),
         axis=1, keepdims=True,
     ).astype(jnp.int32)
-    device, inner = wanted_row // 256, wanted_row % 256
-    core, there_y, there_z = device % 2, device // 16, (device // 2) % 8
+    device, inner = wanted_row >> 8, wanted_row & 255
+    core, there_y, there_z = device & 1, device >> 4, (device >> 1) & 7
     slot = core * 64 + jnp.where(core == 0, there_y * 8 + there_z, there_z * 8 + there_y)
-    row = slot * 4 + inner // 64
+    row = slot * 4 + (inner >> 6)
     lane = iota((16, 128), 1)
     places = jnp.where(
-        lane == 0, row // 8, jnp.where(lane == 1, row % 8, jnp.where(lane == 2, inner % 64, 0))
+        lane == 0, row >> 3, jnp.where(lane == 1, row & 7, jnp.where(lane == 2, inner & 63, 0))
     ).astype(F32)
     rest = jnp.concatenate([listed, places], axis=1)
-    message = jnp.concatenate(
-        [own4[:, :256], own4[:, 256:512], own4[:, 512:], rest[0:4]], axis=0
-    ).astype(BF16)
-    g0[pl.ds(pl.multiple_of(a * 16, 16), 16), :] = message
-    pl.semaphore_wait(barrier, 2 * (NA - 1) + NX)
-
     own = g0.at[pl.ds(pl.multiple_of(a * 16, 16), 16), :]
-    for k in ORDER:
-        send(own, own, ag1_ss.at[k], ag1_rs.at[k], on_a(k)[1])
+    g0[pl.ds(pl.multiple_of(a * 16, 16), 16), :] = rest.astype(BF16)
+    for k in ORDER:
+        send(own, own, x_ss.at[k], x_rs.at[k], on_a(k)[1])
 
     for load in loads[3:]:
         load.wait()
@@ -180,22 +179,25 @@
         key_len[rows, :] = jnp.broadcast_to(length, (128, 128))
 
     for k in ORDER:
+        arrived(gt.at[on_a(NA - k)[0]], ag1_rs.at[k])
+
+    def widen(g, ss, rs):
+        for k in ORDER:
+            send(g.at[0, b], g.at[0, b], ss.at[8 + k], rs.at[8 + k], on_b(k)[1])
+        send(g.at[0, b], g.at[1, b], ss.at[16], rs.at[16], partner)
+
+    g1[0, b] = jnp.concatenate([gt[i].astype(F32) for i in range(NA)], axis=0).astype(BF16)
+    widen(g1, ag1_ss, ag1_rs)
+    for k in ORDER:
         place = on_a(NA - k)[0]
-        arrived(g0.at[pl.ds(pl.multiple_of(place * 16, 16), 16), :], ag1_rs.at[k])
-
-    unfold = fold_matrix()
-    g1[0, b] = dot(unfold, g0[...]).astype(BF16)
-    text_of = lambda region, place: g1.at[region, place, pl.ds(0, 96), :]
-    ids_of = lambda region, place: g1.at[region, place, pl.ds(96, 32), :]
-    for part, ss, rs in ((text_of, ag1_ss, ag1_rs), (ids_of, x_ss, x_rs)):
-        for k in ORDER:
-            send(part(0, b), part(0, b), ss.at[8 + k], rs.at[8 + k], on_b(k)[1])
-        send(part(0, b), part(1, b), ss.at[16], rs.at[16], partner)
-
-    def forward(part, ss, rs, k):
+        arrived(g0.at[pl.ds(pl.multiple_of(place * 16, 16), 16), :], x_rs.at[k])
+    gx[0, b] = dot(spread_matrix(), g0[...]).astype(BF16)
+    widen(gx, x_ss, x_rs)
+
+    def forward(g, ss, rs, k):
         place = on_b(NA - k)[0]
-        arrived(part(0, place), rs.at[8 + k])
-        send(part(0, place), part(1, place), ss.at[16 + k], rs.at[16 + k], partner)
+        arrived(g.at[0, place], rs.at[8 + k])
+        send(g.at[0, place], g.at[1, place], ss.at[16 + k], rs.at[16 + k], partner)
 
     def from_core(k):
         return lax.rem(a + NA - k, NA) if k else a
@@ -203,9 +205,7 @@
     def query_block(region, places):
         shifts = []
         for place in places:
-            block = g1[region, place, 0:96, :].astype(F32)
-            features = jnp.concatenate([block[0:32], block[32:64], block[64:96]], axis=1)
-            normed, spread, shifted = normalise(features, gain, bias)
+            normed, spread, shifted = normalise(g1[region, place].astype(F32), gain, bias)
             rows = pl.ds(pl.multiple_of(region * 256 + place * 32, 32), 32)
             normed_all[rows, :] = normed
             shifted_all[rows, :] = shifted
@@ -223,34 +223,32 @@
 
     near, far = ORDER[:3], ORDER[3:]
     for k in near:
-        forward(text_of, ag1_ss, ag1_rs, k)
+        forward(g1, ag1_ss, ag1_rs, k)
     query_block(0, [b] + [on_b(NA - k)[0] for k in near])
     for k in (0,) + near:
-        arrived(text_of(1, from_core(k)), ag1_rs.at[16 + k])
+        arrived(g1.at[1, from_core(k)], ag1_rs.at[16 + k])
     query_block(1, [from_core(k) for k in (0,) + near])
     for k in far:
-        forward(text_of, ag1_ss, ag1_rs, k)
+        forward(g1, ag1_ss, ag1_rs, k)
     query_block(0, [on_b(NA - k)[0] for k in far])
     for k in ORDER:
-        forward(ids_of, x_ss, x_rs, k)
+        forward(gx, x_ss, x_rs, k)
     for k in far:
-        arrived(text_of(1, from_core(k)), ag1_rs.at[16 + k])
+        arrived(g1.at[1, from_core(k)], ag1_rs.at[16 + k])
     query_block(1, [from_core(k) for k in far])
     for k in (0,) + ORDER:
-        arrived(ids_of(1, from_core(k)), x_rs.at[16 + k])
+        arrived(gx.at[1, from_core(k)], x_rs.at[16 + k])
 
     for region in range(2):
         for i in range(2):
-            table = jnp.concatenate(
-                [g1[region, i * 4 + j, 96:128, :] for j in range(4)], axis=0
-            ).astype(F32)
+            table = gx[region, i * 4:i * 4 + 4].reshape(128, 256).astype(F32)
             first = region * 256 + i * 128
             xt[:, first:first + 128] = table.T
 
     high = xt[128:129, :].astype(jnp.int32)
     low = xt[129:130, :].astype(jnp.int32)
     lane = xt[130:131, :].astype(jnp.int32)
-    slot = lax.rem(high * 8 + low + 256 * c, 512)
+    slot = (high * 8 + low + 256 * c) & 511
     choose = jnp.where(iota((512, 512), 0) == slot, F32(1.0), F32(0.0)).astype(BF16)
     found = dot(xt[0:128, :].astype(BF16), choose)
     where_row = iota((128, 512), 0)
@@ -298,15 +296,18 @@
 
     @pl.loop(0, NA)
     def _(i):
-        rows = pl.ds(pl.multiple_of(i * 32, 32), 32)
-        for part in range(2):
-            qb_send[i, part] = (
-                q_own[part, rows, :] + q_core[part, rows, :].astype(F32)
-            ).astype(BF16)
-
-    for k in ORDER:
-        there, device = on_b(k)
-        send(qb_send.at[there], qb_recv.at[b], q_ss.at[8 + k], q_rs.at[8 + k], device)
+        for h in range(2):
+            rows = pl.ds(pl.multiple_of(i * 32 + h * 16, 16), 16)
+            for part in range(2):
+                qb_send[i, h, part] = (
+                    q_own[part, rows, :] + q_core[part, rows, :].astype(F32)
+                ).astype(BF16)
+
+    for h in range(2):
+        for k in ORDER:
+            there, device = on_b(k)
+            send(qb_send.at[there, h], qb_recv.at[b, h],
+                 q_ss.at[8 + 8 * h + k], q_rs.at[8 + 8 * h + k], device)
     qb_recv[b] = qb_send[b]
 
     for k in ORDER:
@@ -321,12 +322,12 @@
     ).astype(BF16)
     emb_sel[...] = dot(emb_ref[...], pick).astype(BF16)
     place = iota((1, 1024), 1)
-    core = lax.rem(place // 512 + c, 2)
-    place_b, place_a = (place // 64) % 8, (place // 8) % 8
+    core = ((place >> 9) + c) & 1
+    place_b, place_a = (place >> 6) & 7, (place >> 3) & 7
     place_y = jnp.where(core == 0, place_b, place_a)
     place_z = place_a + place_b - place_y
     column = jnp.where(
-        place % 8 < 6, 6 * (place_y * 16 + place_z * 2 + core) + place % 8, -1
+        (place & 7) < 6, 6 * (place_y * 16 + place_z * 2 + core) + (place & 7), -1
     )
 
     @pl.loop(0, D // 128)
@@ -360,26 +361,27 @@
         send(k_send.at[there], k_recv.at[x], k_ss.at[k], k_rs.at[k], device)
     k_recv[x] = k_send[x]
 
-    diagonal = iota((32, SLAB), 1) == iota((32, SLAB), 0) + b * 32
-
-    def as_column(rows):
+    def as_column(rows, h):
         wide = jnp.concatenate([rows[0:1], rows[1:2]], axis=1)
+        diagonal = iota((16, SLAB), 1) == iota((16, SLAB), 0) + (b * 32 + h * 16)
         return jnp.sum(jnp.where(diagonal, wide, F32(0.0)), axis=1, keepdims=True)
 
-    for k in ORDER:
-        arrived(qb_recv.at[on_b(NA - k)[0]], q_rs.at[8 + k])
-    sums = []
-    for part in range(2):
-        total = qb_recv[0, part].astype(F32)
-        for i in range(1, NA):
-            total = total + qb_recv[i, part].astype(F32)
-        sums.append(total)
-    qa_recv[a] = (
-        sums[0] * as_column(by_total)
-        - (sums[1] * as_column(by_positive)) * as_column(share_negative)
-    ).astype(BF16)
-    for k in ORDER:
-        send(qa_recv.at[a], qa_recv.at[a], q_ss.at[16 + k], q_rs.at[16 + k], on_a(k)[1])
+    for h in range(2):
+        for k in ORDER:
+            arrived(qb_recv.at[on_b(NA - k)[0], h], q_rs.at[8 + 8 * h + k])
+        sums = []
+        for part in range(2):
+            total = qb_recv[0, h, part].astype(F32)
+            for i in range(1, NA):
+                total = total + qb_recv[i, h, part].astype(F32)
+            sums.append(total)
+        qa_recv[h, a] = (
+            sums[0] * as_column(by_total, h)
+            - (sums[1] * as_column(by_positive, h)) * as_column(share_negative, h)
+        ).astype(BF16)
+        for k in ORDER:
+            send(qa_recv.at[h, a], qa_recv.at[h, a],
+                 q_ss.at[24 + 8 * h + k], q_rs.at[24 + 8 * h + k], on_a(k)[1])
 
     for k in XORDER:
         arrived(k_recv.at[on_x(NX - k)[0]], k_rs.at[k])
@@ -390,10 +392,27 @@
     unit = unit_key[quarter, :]
     krg[x] = (
         (key_sum - unit * jnp.sum(unit * key_sum, axis=1, keepdims=True))
-        / key_len[quarter, 0:1]
+        * (1.0 / key_len[quarter, 0:1])
     ).astype(BF16)
     for k in XORDER:
         send(krg.at[x], krg.at[x], k_ss.at[4 + k], k_rs.at[4 + k], on_x(k)[1])
+
+    for h in range(2):
+        for k in ORDER:
+            arrived(qa_recv.at[h, on_a(NA - k)[0]], q_rs.at[24 + 8 * h + k])
+        query_sum = qa_recv[h, 0].astype(F32)
+        for i in range(1, NA):
+            query_sum = query_sum + qa_recv[h, i].astype(F32)
+        rows = pl.ds(pl.multiple_of(b * 32 + h * 16, 16), 16)
+        unit = unit_all[rows, :]
+        g2[0, b, h] = (
+            (query_sum - unit * jnp.sum(unit * query_sum, axis=1, keepdims=True))
+            * (1.0 / len_all[rows, 0:1])
+        ).astype(BF16)
+        for k in ORDER:
+            send(g2.at[0, b, h], g2.at[0, b, h],
+                 ag2_ss.at[8 * h + k], ag2_rs.at[8 * h + k], on_b(k)[1])
+        send(g2.at[0, b, h], g2.at[1, b, h], ag2_ss.at[16 + 8 * h], ag2_rs.at[16 + 8 * h], partner)
 
     for k in XORDER:
         arrived(krg.at[on_x(NX - k)[0]], k_rs.at[4 + k])
@@ -411,22 +430,6 @@
     s_send[...] = s_own[512:1024, :].astype(BF16)
     send(s_send, s_core, s_ss.at[0], s_rs.at[0], partner)
 
-    for k in ORDER:
-        arrived(qa_recv.at[on_a(NA - k)[0]], q_rs.at[16 + k])
-    query_sum = qa_recv[0].astype(F32)
-    for i in range(1, NA):
-        query_sum = query_sum + qa_recv[i].astype(F32)
-    block = pl.ds(pl.multiple_of(b * 32, 32), 32)
-    unit = unit_all[block, :]
-    qrg = (
-        (query_sum - unit * jnp.sum(unit * query_sum, axis=1, keepdims=True))
-        / len_all[block, 0:1]
-    ).astype(BF16)
-    g2[0, b] = qrg
-    for k in ORDER:
-        send(g2.at[0, b], g2.at[0, b], ag2_ss.at[k], ag2_rs.at[k], on_b(k)[1])
-    send(g2.at[0, b], g2.at[1, b], ag2_ss.at[8], ag2_rs.at[8], partner)
-
     arrived(s_core, s_rs.at[0])
     for i in range(NA):
         rows = slice(i * 64, i * 64 + 64)
@@ -436,18 +439,41 @@
         send(sb_send.at[there], sb_recv.at[b], s_ss.at[8 + k], s_rs.at[8 + k], device)
     sb_recv[b] = sb_send[b]
 
-    shifted_grad = dot_cols(qrg, proj_ref[...])
+    shifted_grad = dot_cols(g2[0, b].reshape(32, D), proj_ref[...])
+    block = pl.ds(pl.multiple_of(b * 32, 32), 32)
     scaled = shifted_grad * gain
     normed = normed_all[block, :]
     text = (
         scaled
         - jnp.mean(scaled, axis=1, keepdims=True)
         - normed * jnp.mean(scaled * normed, axis=1, keepdims=True)
-    ) / spread_all[block, 0:1]
+    ) * (1.0 / spread_all[block, 0:1])
     own_text = text[0:4]
     for i in range(1, NA):
         own_text = jnp.where(a == i, text[i * 4:i * 4 + 4], own_text)
-    text_out[...] = own_text
+    small_out[0:4, :] = own_text
+
+    for h in range(2):
+        for k in ORDER:
+            place = on_b(NA - k)[0]
+            arrived(g2.at[0, place, h], ag2_rs.at[8 * h + k])
+            send(g2.at[0, place, h], g2.at[1, place, h],
+                 ag2_ss.at[16 + 8 * h + k], ag2_rs.at[16 + 8 * h + k], partner)
+    for h in range(2):
+        for k in (0,) + ORDER:
+            arrived(g2.at[1, from_core(k), h], ag2_rs.at[16 + 8 * h + k])
+
+    cols = pl.ds(pl.multiple_of(c * 384, 128), 384)
+    half = g2[:, :, :, :, cols].reshape(GROUP, 384)
+    for i in range(D // 128):
+        band = slice(i * 128, i * 128 + 128)
+        p_send[band, :] = dot_rows(shifted_all[:, band], half).astype(BF16)
+    for h in range(2):
+        for k in XORDER:
+            there, device = on_x(k)
+            send(p_send.at[pl.ds(pl.multiple_of(there * 192 + h * 96, 32), 96), :],
+                 p_recv.at[h, x], p_ss.at[4 * h + k], p_rs.at[4 * h + k], device)
+        p_recv[h, x] = p_send[pl.ds(pl.multiple_of(x * 192 + h * 96, 32), 96), :]
 
     for k in ORDER:
         arrived(sb_recv.at[on_b(NA - k)[0]], s_rs.at[8 + k])
@@ -460,32 +486,6 @@
         there, device = on_a(k)
         send(sa_send.at[there], sa_recv.at[a], s_ss.at[k], s_rs.at[k], device)
     sa_recv[a] = sa_send[a]
-
-    for k in ORDER:
-        place = on_b(NA - k)[0]
-        arrived(g2.at[0, place], ag2_rs.at[k])
-        send(g2.at[0, place], g2.at[1, place], ag2_ss.at[8 + k], ag2_rs.at[8 + k], partner)
-
-    for k in ORDER:
-        arrived(sa_recv.at[on_a(NA - k)[0]], s_rs.at[k])
-    s_wide[...] = jnp.zeros((128, 256), F32)
-    s_wide[0:8, :] = jnp.sum(sa_recv[...], axis=0)
-    adapter_out[...] = s_wide[...].T[0:192, 0:6]
-
-    for k in (0,) + ORDER:
-        arrived(g2.at[1, from_core(k)], ag2_rs.at[8 + k])
-
-    cols = pl.ds(pl.multiple_of(c * 384, 128), 384)
-    half = g2[:, :, :, cols].reshape(GROUP, 384)
-    for i in range(D // 128):
-        band = slice(i * 128, i * 128 + 128)
-        p_send[band, :] = dot_rows(shifted_all[:, band], half).astype(BF16)
-    for h in range(2):
-        for k in XORDER:
-            there, device = on_x(k)
-            send(p_send.at[pl.ds(pl.multiple_of(there * 192 + h * 96, 32), 96), :],
-                 p_recv.at[h, x], p_ss.at[4 * h + k], p_rs.at[4 * h + k], device)
-        p_recv[h, x] = p_send[pl.ds(pl.multiple_of(x * 192 + h * 96, 32), 96), :]
 
     gain_sum = jnp.zeros((1, D), F32)
     bias_sum = jnp.zeros((1, D), F32)
@@ -513,7 +513,11 @@
 
     for k in XORDER:
         arrived(gb_recv.at[on_x(NX - k)[0]], p_rs.at[8 + k])
-    gb_out[...] = jnp.sum(gb_recv[...], axis=0)
+    small_out[4:6, :] = jnp.sum(gb_recv[...], axis=0)[0:2]
+
+    for k in ORDER:
+        arrived(sa_recv.at[on_a(NA - k)[0]], s_rs.at[k])
+    small_out[8:16, 0:256] = jnp.sum(sa_recv[...], axis=0)
 
     for h in range(2):
         for k in XORDER:
@@ -541,16 +545,14 @@
 ):
     whole = pl.BlockSpec(memory_space=pltpu.VMEM)
     dma = pltpu.SemaphoreType.DMA
-    text_grad, gain_bias, projection_grad, adapter_grad = pl.pallas_call(
+    small, projection_grad = pl.pallas_call(
         kernel,
         out_shape=(
-            jax.ShapeDtypeStruct((ROWS, D), F32),
-            jax.ShapeDtypeStruct((8, D), F32),
+            jax.ShapeDtypeStruct((16, D), F32),
             jax.ShapeDtypeStruct((D, D), BF16),
-            jax.ShapeDtypeStruct((192, 6), F32),
         ),
         in_specs=[pl.BlockSpec(memory_space=pl.ANY)] * 8,
-        out_specs=(whole,) * 4,
+        out_specs=(whole,) * 2,
         scratch_shapes=[
             pltpu.VMEM((ROWS, D), BF16),
             pltpu.VMEM((D,), F32),
@@ -560,9 +562,11 @@
             pltpu.VMEM((D, D), BF16),
             pltpu.VMEM((SLAB,), jnp.int32),
             pltpu.VMEM((ROWS,), jnp.int32),
+            pltpu.VMEM((NA, ROWS, D), BF16),
             pltpu.VMEM((128, 256), BF16),
-            pltpu.VMEM((2, NA, 128, 256), BF16),
             pltpu.VMEM((2, NA, 32, D), BF16),
+            pltpu.VMEM((2, NA, 32, 256), BF16),
+            pltpu.VMEM((2, NA, 2, 16, D), BF16),
             pltpu.VMEM((SLAB, D), F32),
             pltpu.VMEM((SLAB, D), BF16),
             pltpu.VMEM((SLAB, 128), F32),
@@ -587,9 +591,9 @@
             pltpu.VMEM((2, 256, D), BF16),
             pltpu.VMEM((2, 256, D), F32),
             pltpu.VMEM((2, 256, D), BF16),
-            pltpu.VMEM((NA, 2, 32, D), BF16),
-            pltpu.VMEM((NA, 2, 32, D), BF16),
-            pltpu.VMEM((NA, 32, D), BF16),
+            pltpu.VMEM((NA, 2, 2, 16, D), BF16),
+            pltpu.VMEM((NA, 2, 2, 16, D), BF16),
+            pltpu.VMEM((2, NA, 16, D), BF16),
             pltpu.VMEM((NX, 64, D), BF16),
             pltpu.VMEM((NX, 64, D), BF16),
             pltpu.VMEM((NX, 64, D), BF16),
@@ -600,7 +604,6 @@
             pltpu.VMEM((NA, 64, 256), BF16),
             pltpu.VMEM((NA, 8, 256), F32),
             pltpu.VMEM((NA, 8, 256), F32),
-            pltpu.VMEM((128, 256), F32),
             pltpu.VMEM((D, 384), BF16),
             pltpu.VMEM((2, NX, 96, 384), BF16),
             pltpu.VMEM((2, NX, 2, 96, 384), BF16),
@@ -608,15 +611,15 @@
             dma((24,)), dma((24,)),
             dma((24,)), dma((24,)),
             dma((16,)), dma((16,)),
-            dma((24,)), dma((24,)),
-            dma((16,)), dma((16,)),
+            dma((40,)), dma((40,)),
+            dma((32,)), dma((32,)),
             dma((8,)), dma((8,)),
             dma((16,)), dma((16,)),
             dma((28,)), dma((28,)),
             dma((8,)),
         ],
         compiler_params=pltpu.CompilerParams(
-            collective_id=0, has_side_effects=True, vmem_limit_bytes=48 * 1024 * 1024
+            collective_id=0, has_side_effects=True, vmem_limit_bytes=62 * 1024 * 1024
         ),
     )(
         text_features,
@@ -628,7 +631,7 @@
         slab_ids,
         positive_rows,
     )
-    return text_grad, gain_bias[0], gain_bias[1], projection_grad, adapter_grad
+    return small[0:4], small[4], small[5], projection_grad, small[8:14, 0:192].T
 
 
 def solution(mesh):

time: 110 us -> 96.8 us (0.88)
  Pallas kernels: 99.5 us -> 89.4 us
  local copies, waits for them, and re-layouts: 9.83 us -> 6.42 us
    pallas_call x1, Pallas kernels: 99.5 us -> 89.4 us  [shards(): pl.pallas_call(kernel, out_shape=(jax.ShapeDtypeStruct((16, D), F32), jax...]
    unnamed x19 -> x1, local copies, waits for them, and re-layouts: 9.22 us -> 2.36 us
    slice x1 -> x2, local copies, waits for them, and re-layouts: 0.61 us -> 2.77 us  [the longest x1 1.43 us: shards(): small[5]]
    transpose x0 -> x1, local copies, waits for them, and re-layouts: none -> 1.29 us  [shards(): small[8:14, 0:192]]
where the time goes in v3:
time: 96.8 us; the launch traced here: 96.5 us
  Pallas kernels  89.4 us (92%)
  local copies, waits for them, and re-layouts  6.42 us (7%)
    pallas_call x1, Pallas kernels, shards(): pl.pallas_call(kernel, out_shape=(jax.ShapeDtypeStruct((16, D), F32), jax...  89.4 us
    unnamed x1, local copies, waits for them, and re-layouts  2.36 us

profile of v3, /device:TPU:1, one launch (start us, length us, event | category | flops | bytes accessed | tf_op | source)
XLA Modules:
  0.0 96.5 jit_solution(13432321213432460896)
XLA Ops:
  0.6 89.4 %shard_map.119 = (f32[16,768]{1,0:T(8,128)}, bf16[768,768]{1,0:T(8,128)(2,1)}) custom-call(bf16[4,768]{1,0:T(4,128)(2,1)} %tf_hbm.1, f32[768]{0:T(1024)} %gain_hbm.1, f32[768]{0:T(1024)} %bias_hbm.1, bf16[768,768]{1,0:T(8,128)(2,1)} %proj_hbm.1, bf16[256,768]{1,0:T(8,128)(2,1)} %emb_hbm.1, bf16[768,768]{1,0:T(8,128)(2,1)} %adapter_hbm.1, s32[256]{0:T(256)} %ids_hbm.1, ...), custom_call_target="tpu_custom_call" | custom-call | tf_op jit(solution)/shard_map/pallas_call | solution.py:548
  90.1 1.4 %slice_reduce_fusion = (f32[768]{0:T(1024)}, f32[768]{0:T(1024)}) fusion(f32[16,768]{1,0:T(8,128)} %get-tuple-element.7), kind=kLoop, calls=%fused_computation.1 | loop fusion | bytes 12288 | tf_op jit(solution)/shard_map/slice | solution.py:634
  91.5 1.3 %slice.12 = f32[4,768]{1,0:T(4,128)} slice(f32[16,768]{1,0:T(8,128)} %get-tuple-element.7), slice={[0:4], [0:768]} | slice | bytes 24576 | tf_op jit(solution)/shard_map/slice | solution.py:634
  92.8 1.3 %slice_bitcast_fusion = f32[192,6]{0,1:T(8,128)} fusion(f32[16,768]{1,0:T(8,128)} %get-tuple-element.7), kind=kLoop, calls=%fused_computation | loop fusion | bytes 9216 | tf_op jit(solution)/shard_map/transpose | solution.py:634
  94.1 2.4 %copy.14 = bf16[768,768]{1,0:T(8,128)(2,1)} copy(bf16[768,768]{1,0:T(8,128)(2,1)} %get-tuple-element.19) | data formatting | bytes 2359296

commit v4 on v3

--- a/solution.py
+++ b/solution.py
@@ -58,7 +58,7 @@
 def kernel(
     tf_hbm, gain_hbm, bias_hbm, proj_hbm, emb_hbm, adapter_hbm, ids_hbm, rows_hbm,
     small_out, proj_out,
-    tf_ref, gain_ref, bias_ref, proj_ref, emb_ref, adapter_ref, ids_ref, rows_ref,
+    gain_ref, bias_ref, proj_ref, emb_ref, adapter_ref, ids_ref, rows_ref,
     gt, g0, g1, gx, g2, unit_key, key_half, key_len, emb_sel, perm,
     normed_all, shifted_all, query_half, unit_all, len_all, spread_all, xt,
     negs, poss, negs_half, poss_half, weights,
@@ -67,7 +67,7 @@
     k_send, k_recv, krg, s_own, s_send, s_core, sb_send, sb_recv, sa_send, sa_recv,
     p_send, p_recv, p_out, gb_recv,
     ag1_ss, ag1_rs, x_ss, x_rs, st_ss, st_rs, q_ss, q_rs, ag2_ss, ag2_rs, k_ss, k_rs,
-    s_ss, s_rs, p_ss, p_rs, in_sem,
+    s_ss, s_rs, p_ss, p_rs, in_sem, out_sem,
 ):
     corpus = lax.axis_index("corpus")
     x = lax.axis_index("query")
@@ -119,7 +119,7 @@
     loads = [
         pltpu.make_async_copy(src, dst, in_sem.at[i])
         for i, (src, dst) in enumerate((
-            (tf_hbm, tf_ref), (ids_hbm, ids_ref), (rows_hbm, rows_ref), (emb_hbm, emb_ref),
+            (tf_hbm, gt.at[a]), (ids_hbm, ids_ref), (rows_hbm, rows_ref), (emb_hbm, emb_ref),
             (adapter_hbm, adapter_ref), (gain_hbm, gain_ref), (bias_hbm, bias_ref),
             (proj_hbm, proj_ref),
         ))
@@ -127,11 +127,9 @@
     for load in loads:
         load.start()
 
-    loads[0].wait()
-    gt[a] = tf_ref[...]
     pl.semaphore_wait(barrier, 2 * (NA - 1) + NX)
     for k in ORDER:
-        send(gt.at[a], gt.at[a], ag1_ss.at[k], ag1_rs.at[k], on_a(k)[1])
+        send(tf_hbm, gt.at[a], ag1_ss.at[k], ag1_rs.at[k], on_a(k)[1])
 
     for load in loads[1:3]:
         load.wait()
@@ -184,10 +182,11 @@
     def widen(g, ss, rs):
         for k in ORDER:
             send(g.at[0, b], g.at[0, b], ss.at[8 + k], rs.at[8 + k], on_b(k)[1])
-        send(g.at[0, b], g.at[1, b], ss.at[16], rs.at[16], partner)
-
+
+    loads[0].wait()
     g1[0, b] = jnp.concatenate([gt[i].astype(F32) for i in range(NA)], axis=0).astype(BF16)
     widen(g1, ag1_ss, ag1_rs)
+    send(g1.at[0, b], g1.at[1, b], ag1_ss.at[16], ag1_rs.at[16], partner)
     for k in ORDER:
         place = on_a(NA - k)[0]
         arrived(g0.at[pl.ds(pl.multiple_of(place * 16, 16), 16), :], x_rs.at[k])
@@ -232,12 +231,12 @@
         forward(g1, ag1_ss, ag1_rs, k)
     query_block(0, [on_b(NA - k)[0] for k in far])
     for k in ORDER:
-        forward(gx, x_ss, x_rs, k)
+        arrived(gx.at[0, on_b(NA - k)[0]], x_rs.at[8 + k])
+    send(gx.at[0], gx.at[1], x_ss.at[16], x_rs.at[16], partner)
     for k in far:
         arrived(g1.at[1, from_core(k)], ag1_rs.at[16 + k])
     query_block(1, [from_core(k) for k in far])
-    for k in (0,) + ORDER:
-        arrived(gx.at[1, from_core(k)], x_rs.at[16 + k])
+    arrived(gx.at[1], x_rs.at[16])
 
     for region in range(2):
         for i in range(2):
@@ -294,16 +293,16 @@
     for part in range(2):
         arrived(q_core.at[part], q_rs.at[part])
 
-    @pl.loop(0, NA)
-    def _(i):
-        for h in range(2):
+    for h in range(2):
+
+        @pl.loop(0, NA)
+        def _(i):
             rows = pl.ds(pl.multiple_of(i * 32 + h * 16, 16), 16)
             for part in range(2):
                 qb_send[i, h, part] = (
                     q_own[part, rows, :] + q_core[part, rows, :].astype(F32)
                 ).astype(BF16)
 
-    for h in range(2):
         for k in ORDER:
             there, device = on_b(k)
             send(qb_send.at[there, h], qb_recv.at[b, h],
@@ -499,6 +498,21 @@
     for k in XORDER:
         send(gb_recv.at[x], gb_recv.at[x], p_ss.at[8 + k], p_rs.at[8 + k], on_x(k)[1])
 
+    stores = []
+
+    def store(side, place, h, i):
+        rows = pl.ds(pl.multiple_of(place * 192 + h * 96, 32), 96)
+        lanes = pl.ds(pl.multiple_of((c + side * (1 - 2 * c)) * 384, 128), 384)
+        copy = pltpu.make_async_copy(
+            p_out.at[side, place, h], proj_out.at[rows, lanes], out_sem.at[i]
+        )
+        copy.start()
+        stores.append(copy)
+
+    for copy in pending[:-30]:
+        copy.wait_send()
+    del pending[:-30]
+
     for h in range(2):
         for k in XORDER:
             arrived(p_recv.at[h, on_x(NX - k)[0]], p_rs.at[4 * h + k])
@@ -510,6 +524,7 @@
             send(p_out.at[0, x, h], p_out.at[0, x, h],
                  p_ss.at[12 + 4 * h + k], p_rs.at[12 + 4 * h + k], on_x(k)[1])
         send(p_out.at[0, x, h], p_out.at[1, x, h], p_ss.at[20 + 4 * h], p_rs.at[20 + 4 * h], partner)
+        store(0, x, h, 4 * h)
 
     for k in XORDER:
         arrived(gb_recv.at[on_x(NX - k)[0]], p_rs.at[8 + k])
@@ -525,18 +540,52 @@
             arrived(p_out.at[0, there, h], p_rs.at[12 + 4 * h + k])
             send(p_out.at[0, there, h], p_out.at[1, there, h],
                  p_ss.at[20 + 4 * h + k], p_rs.at[20 + 4 * h + k], partner)
-    for i in range(NX):
-        proj_out[i * 192:i * 192 + 192, cols] = p_out[0, i].reshape(192, 384)
-    other = pl.ds(pl.multiple_of((1 - c) * 384, 128), 384)
+            store(0, there, h, 4 * h + k)
     for h in range(2):
         arrived(p_out.at[1, x, h], p_rs.at[20 + 4 * h])
+        store(1, x, h, 8 + 4 * h)
         for k in XORDER:
-            arrived(p_out.at[1, on_x(NX - k)[0], h], p_rs.at[20 + 4 * h + k])
-    for i in range(NX):
-        proj_out[i * 192:i * 192 + 192, other] = p_out[1, i].reshape(192, 384)
-
+            there = on_x(NX - k)[0]
+            arrived(p_out.at[1, there, h], p_rs.at[20 + 4 * h + k])
+            store(1, there, h, 8 + 4 * h + k)
+    for copy in stores:
+        copy.wait()
     for copy in pending:
         copy.wait_send()
+
+
+def finish(
+    small_hbm, part_hbm, text_hbm, gain_hbm, bias_hbm, proj_hbm, adapter_hbm,
+    small, held, text, gain, bias, adapter, in_sem, out_sem,
+):
+    bands = [pl.ds(i * 192, 192) for i in range(4)]
+    into = [pltpu.make_async_copy(small_hbm, small, in_sem.at[0])] + [
+        pltpu.make_async_copy(part_hbm.at[band], held.at[band], in_sem.at[1 + i])
+        for i, band in enumerate(bands)
+    ]
+    out = [
+        pltpu.make_async_copy(held.at[band], proj_hbm.at[band], out_sem.at[i])
+        for i, band in enumerate(bands)
+    ] + [
+        pltpu.make_async_copy(src, dst, out_sem.at[4 + i])
+        for i, (src, dst) in enumerate((
+            (text, text_hbm), (gain, gain_hbm), (bias, bias_hbm), (adapter, adapter_hbm)
+        ))
+    ]
+    for copy in into:
+        copy.start()
+    into[0].wait()
+    text[...] = small[0:4, :]
+    gain[...] = small[4:5, :].reshape(D)
+    bias[...] = small[5:6, :].reshape(D)
+    adapter[...] = small[8:14, 0:192]
+    for copy in out[4:]:
+        copy.start()
+    for first, second in zip(into[1:], out[:4]):
+        first.wait()
+        second.start()
+    for copy in out:
+        copy.wait()
 
 
 def shards(
@@ -552,9 +601,8 @@
             jax.ShapeDtypeStruct((D, D), BF16),
         ),
         in_specs=[pl.BlockSpec(memory_space=pl.ANY)] * 8,
-        out_specs=(whole,) * 2,
+        out_specs=(whole, pl.BlockSpec(memory_space=pl.ANY)),
         scratch_shapes=[
-            pltpu.VMEM((ROWS, D), BF16),
             pltpu.VMEM((D,), F32),
             pltpu.VMEM((D,), F32),
             pltpu.VMEM((D, D), BF16),
@@ -616,7 +664,7 @@
             dma((8,)), dma((8,)),
             dma((16,)), dma((16,)),
             dma((28,)), dma((28,)),
-            dma((8,)),
+            dma((8,)), dma((16,)),
         ],
         compiler_params=pltpu.CompilerParams(
             collective_id=0, has_side_effects=True, vmem_limit_bytes=62 * 1024 * 1024
@@ -631,7 +679,29 @@
         slab_ids,
         positive_rows,
     )
-    return small[0:4], small[4], small[5], projection_grad, small[8:14, 0:192].T
+    text_grad, gain_grad, bias_grad, projection_grad, adapter_grad = pl.pallas_call(
+        finish,
+        out_shape=(
+            jax.ShapeDtypeStruct((ROWS, D), F32),
+            jax.ShapeDtypeStruct((D,), F32),
+            jax.ShapeDtypeStruct((D,), F32),
+            jax.ShapeDtypeStruct((D, D), BF16),
+            jax.ShapeDtypeStruct((6, 192), F32),
+        ),
+        in_specs=[pl.BlockSpec(memory_space=pl.ANY)] * 2,
+        out_specs=(pl.BlockSpec(memory_space=pl.ANY),) * 5,
+        scratch_shapes=[
+            pltpu.VMEM((16, D), F32),
+            pltpu.VMEM((D, D), BF16),
+            pltpu.VMEM((ROWS, D), F32),
+            pltpu.VMEM((D,), F32),
+            pltpu.VMEM((D,), F32),
+            pltpu.VMEM((6, 192), F32),
+            dma((5,)), dma((8,)),
+        ],
+        compiler_params=pltpu.CompilerParams(vmem_limit_bytes=62 * 1024 * 1024),
+    )(small, projection_grad)
+    return text_grad, gain_grad, bias_grad, projection_grad, adapter_grad.T
 
 
 def solution(mesh):

time: 96.8 us -> 92.6 us (0.957)
  local copies, waits for them, and re-layouts: 6.42 us -> 0 us
  Pallas kernels: 89.4 us -> 91.8 us
    slice x2 -> x0, local copies, waits for them, and re-layouts: 2.77 us -> none  [the longest x1 1.43 us: shards(): small[5]]
    unnamed x1 -> x0, local copies, waits for them, and re-layouts: 2.36 us -> none
    pallas_call x0 -> x1, Pallas kernels: none -> 2.12 us  [shards(): pl.pallas_call(finish, out_shape=(jax.ShapeDtypeStruct((ROWS, D), F32), j...]
    transpose x1 -> x0, local copies, waits for them, and re-layouts: 1.29 us -> none  [shards(): small[8:14, 0:192]]
where the time goes in v4:
time: 92.6 us; the launch traced here: 92.4 us
  Pallas kernels  91.8 us (99%)
    pallas_call x1, Pallas kernels, shards(): pl.pallas_call(kernel, out_shape=(jax.ShapeDtypeStruct((16, D), F32), jax...  89.7 us
    pallas_call x1, Pallas kernels, shards(): pl.pallas_call(finish, out_shape=(jax.ShapeDtypeStruct((ROWS, D), F32), j...  2.12 us

profile of v4, /device:TPU:1, one launch (start us, length us, event | category | flops | bytes accessed | tf_op | source)
XLA Modules:
  0.0 92.4 jit_solution(11966518251863510305)
XLA Ops:
  0.6 89.7 %shard_map.119 = (f32[16,768]{1,0:T(8,128)}, bf16[768,768]{1,0:T(8,128)(2,1)}) custom-call(bf16[4,768]{1,0:T(4,128)(2,1)} %tf_hbm.1, f32[768]{0:T(1024)} %gain_hbm.1, f32[768]{0:T(1024)} %bias_hbm.1, bf16[768,768]{1,0:T(8,128)(2,1)} %proj_hbm.1, bf16[256,768]{1,0:T(8,128)(2,1)} %emb_hbm.1, bf16[768,768]{1,0:T(8,128)(2,1)} %adapter_hbm.1, s32[256]{0:T(256)} %ids_hbm.1, ...), custom_call_target="tpu_custom_call" | custom-call | tf_op jit(solution)/shard_map/pallas_call | solution.py:597
  90.3 2.1 %shard_map.120 = (f32[4,768]{1,0:T(4,128)}, f32[768]{0:T(1024)}, f32[768]{0:T(1024)}, bf16[768,768]{1,0:T(8,128)(2,1)}, f32[6,192]{1,0:T(8,128)}) custom-call(f32[16,768]{1,0:T(8,128)} %get-tuple-element.12.small_hbm, bf16[768,768]{1,0:T(8,128)(2,1)} %get-tuple-element.13.part_hbm), custom_call_target="tpu_custom_call" | custom-call | tf_op jit(solution)/shard_map/pallas_call | solution.py:682

commit v5 on v4

--- a/solution.py
+++ b/solution.py
@@ -343,29 +343,12 @@
     by_positive = 1.0 / stats[4:8]
     share_negative = stats[0:4] * by_total
 
-    for i in range(4):
-        cols = slice(i * 128, i * 128 + 128)
-        weights[:, cols] = (
-            negs[:, cols] * by_total[i:i + 1, :]
-            - (poss[:, cols] * by_positive[i:i + 1, :]) * share_negative[i:i + 1, :]
-        ).astype(BF16)
-
-    @pl.loop(0, NX)
-    def _(i):
-        rows = pl.ds(pl.multiple_of(i * 64, 64), 64)
-        k_send[i] = dot(weights[rows, :], query_half[...]).astype(BF16)
-
-    for k in XORDER:
-        there, device = on_x(k)
-        send(k_send.at[there], k_recv.at[x], k_ss.at[k], k_rs.at[k], device)
-    k_recv[x] = k_send[x]
-
     def as_column(rows, h):
         wide = jnp.concatenate([rows[0:1], rows[1:2]], axis=1)
         diagonal = iota((16, SLAB), 1) == iota((16, SLAB), 0) + (b * 32 + h * 16)
         return jnp.sum(jnp.where(diagonal, wide, F32(0.0)), axis=1, keepdims=True)
 
-    for h in range(2):
+    def combine(h):
         for k in ORDER:
             arrived(qb_recv.at[on_b(NA - k)[0], h], q_rs.at[8 + 8 * h + k])
         sums = []
@@ -381,6 +364,27 @@
         for k in ORDER:
             send(qa_recv.at[h, a], qa_recv.at[h, a],
                  q_ss.at[24 + 8 * h + k], q_rs.at[24 + 8 * h + k], on_a(k)[1])
+
+    combine(0)
+
+    for i in range(4):
+        cols = slice(i * 128, i * 128 + 128)
+        weights[:, cols] = (
+            negs[:, cols] * by_total[i:i + 1, :]
+            - (poss[:, cols] * by_positive[i:i + 1, :]) * share_negative[i:i + 1, :]
+        ).astype(BF16)
+
+    @pl.loop(0, NX)
+    def _(i):
+        rows = pl.ds(pl.multiple_of(i * 64, 64), 64)
+        k_send[i] = dot(weights[rows, :], query_half[...]).astype(BF16)
+
+    for k in XORDER:
+        there, device = on_x(k)
+        send(k_send.at[there], k_recv.at[x], k_ss.at[k], k_rs.at[k], device)
+    k_recv[x] = k_send[x]
+
+    combine(1)
 
     for k in XORDER:
         arrived(k_recv.at[on_x(NX - k)[0]], k_rs.at[k])
@@ -413,31 +417,6 @@
                  ag2_ss.at[8 * h + k], ag2_rs.at[8 * h + k], on_b(k)[1])
         send(g2.at[0, b, h], g2.at[1, b, h], ag2_ss.at[16 + 8 * h], ag2_rs.at[16 + 8 * h], partner)
 
-    for k in XORDER:
-        arrived(krg.at[on_x(NX - k)[0]], k_rs.at[4 + k])
-    grads = krg[...].reshape(SLAB, D)
-
-    @pl.loop(0, 4)
-    def _(i):
-        half = i // 2
-        cols = pl.ds(pl.multiple_of((3 - i) * 256, 256), 256)
-        spread_out = dot(grads, perm[:, cols]).astype(BF16)
-        share = dot_rows(spread_out, emb_sel[...])
-        rows = pl.ds(pl.multiple_of((3 - i) * 256, 256), 256)
-        s_own[rows, :] = share
-
-    s_send[...] = s_own[512:1024, :].astype(BF16)
-    send(s_send, s_core, s_ss.at[0], s_rs.at[0], partner)
-
-    arrived(s_core, s_rs.at[0])
-    for i in range(NA):
-        rows = slice(i * 64, i * 64 + 64)
-        sb_send[i] = (s_own[rows, :] + s_core[rows, :].astype(F32)).astype(BF16)
-    for k in ORDER:
-        there, device = on_b(k)
-        send(sb_send.at[there], sb_recv.at[b], s_ss.at[8 + k], s_rs.at[8 + k], device)
-    sb_recv[b] = sb_send[b]
-
     shifted_grad = dot_cols(g2[0, b].reshape(32, D), proj_ref[...])
     block = pl.ds(pl.multiple_of(b * 32, 32), 32)
     scaled = shifted_grad * gain
@@ -452,12 +431,37 @@
         own_text = jnp.where(a == i, text[i * 4:i * 4 + 4], own_text)
     small_out[0:4, :] = own_text
 
+    for k in XORDER:
+        arrived(krg.at[on_x(NX - k)[0]], k_rs.at[4 + k])
+    grads = krg[...].reshape(SLAB, D)
+
+    @pl.loop(0, 4)
+    def _(i):
+        half = i // 2
+        cols = pl.ds(pl.multiple_of((3 - i) * 256, 256), 256)
+        spread_out = dot(grads, perm[:, cols]).astype(BF16)
+        share = dot_rows(spread_out, emb_sel[...])
+        rows = pl.ds(pl.multiple_of((3 - i) * 256, 256), 256)
+        s_own[rows, :] = share
+
+    s_send[...] = s_own[512:1024, :].astype(BF16)
+    send(s_send, s_core, s_ss.at[0], s_rs.at[0], partner)
+
     for h in range(2):
         for k in ORDER:
             place = on_b(NA - k)[0]
             arrived(g2.at[0, place, h], ag2_rs.at[8 * h + k])
             send(g2.at[0, place, h], g2.at[1, place, h],
                  ag2_ss.at[16 + 8 * h + k], ag2_rs.at[16 + 8 * h + k], partner)
+    arrived(s_core, s_rs.at[0])
+    for i in range(NA):
+        rows = slice(i * 64, i * 64 + 64)
+        sb_send[i] = (s_own[rows, :] + s_core[rows, :].astype(F32)).astype(BF16)
+    for k in ORDER:
+        there, device = on_b(k)
+        send(sb_send.at[there], sb_recv.at[b], s_ss.at[8 + k], s_rs.at[8 + k], device)
+    sb_recv[b] = sb_send[b]
+
     for h in range(2):
         for k in (0,) + ORDER:
             arrived(g2.at[1, from_core(k), h], ag2_rs.at[16 + 8 * h + k])
@@ -474,18 +478,6 @@
                  p_recv.at[h, x], p_ss.at[4 * h + k], p_rs.at[4 * h + k], device)
         p_recv[h, x] = p_send[pl.ds(pl.multiple_of(x * 192 + h * 96, 32), 96), :]
 
-    for k in ORDER:
-        arrived(sb_recv.at[on_b(NA - k)[0]], s_rs.at[8 + k])
-    part = sb_recv[0].astype(F32)
-    for i in range(1, NA):
-        part = part + sb_recv[i].astype(F32)
-    for i in range(NA):
-        sa_send[i] = part[i * 8:i * 8 + 8, :]
-    for k in ORDER:
-        there, device = on_a(k)
-        send(sa_send.at[there], sa_recv.at[a], s_ss.at[k], s_rs.at[k], device)
-    sa_recv[a] = sa_send[a]
-
     gain_sum = jnp.zeros((1, D), F32)
     bias_sum = jnp.zeros((1, D), F32)
     for i in range(4):
@@ -497,6 +489,18 @@
     gb_recv[x] = jnp.concatenate([gain_sum, bias_sum, jnp.zeros((6, D), F32)], axis=0)
     for k in XORDER:
         send(gb_recv.at[x], gb_recv.at[x], p_ss.at[8 + k], p_rs.at[8 + k], on_x(k)[1])
+
+    for k in ORDER:
+        arrived(sb_recv.at[on_b(NA - k)[0]], s_rs.at[8 + k])
+    part = sb_recv[0].astype(F32)
+    for i in range(1, NA):
+        part = part + sb_recv[i].astype(F32)
+    for i in range(NA):
+        sa_send[i] = part[i * 8:i * 8 + 8, :]
+    for k in ORDER:
+        there, device = on_a(k)
+        send(sa_send.at[there], sa_recv.at[a], s_ss.at[k], s_rs.at[k], device)
+    sa_recv[a] = sa_send[a]
 
     stores = []
 

time: 92.6 us -> 90.7 us (0.979)
  Pallas kernels: 91.8 us -> 89.9 us
    pallas_call x1, Pallas kernels: 89.7 us -> 87.8 us  [shards(): pl.pallas_call(kernel, out_shape=(jax.ShapeDtypeStruct((16, D), F32), jax...]
where the time goes in v5:
time: 90.7 us; the launch traced here: 90.5 us
  Pallas kernels  89.9 us (99%)
    pallas_call x1, Pallas kernels, shards(): pl.pallas_call(kernel, out_shape=(jax.ShapeDtypeStruct((16, D), F32), jax...  87.8 us
    pallas_call x1, Pallas kernels, shards(): pl.pallas_call(finish, out_shape=(jax.ShapeDtypeStruct((ROWS, D), F32), j...  2.12 us

profile of v5, /device:TPU:1, one launch (start us, length us, event | category | flops | bytes accessed | tf_op | source)
XLA Modules:
  0.0 90.5 jit_solution(3419702277633159249)
XLA Ops:
  0.6 87.8 %shard_map.119 = (f32[16,768]{1,0:T(8,128)}, bf16[768,768]{1,0:T(8,128)(2,1)}) custom-call(bf16[4,768]{1,0:T(4,128)(2,1)} %tf_hbm.1, f32[768]{0:T(1024)} %gain_hbm.1, f32[768]{0:T(1024)} %bias_hbm.1, bf16[768,768]{1,0:T(8,128)(2,1)} %proj_hbm.1, bf16[256,768]{1,0:T(8,128)(2,1)} %emb_hbm.1, bf16[768,768]{1,0:T(8,128)(2,1)} %adapter_hbm.1, s32[256]{0:T(256)} %ids_hbm.1, ...), custom_call_target="tpu_custom_call" | custom-call | tf_op jit(solution)/shard_map/pallas_call | solution.py:601
  88.4 2.1 %shard_map.120 = (f32[4,768]{1,0:T(4,128)}, f32[768]{0:T(1024)}, f32[768]{0:T(1024)}, bf16[768,768]{1,0:T(8,128)(2,1)}, f32[6,192]{1,0:T(8,128)}) custom-call(f32[16,768]{1,0:T(8,128)} %get-tuple-element.12.small_hbm, bf16[768,768]{1,0:T(8,128)(2,1)} %get-tuple-element.13.part_hbm), custom_call_target="tpu_custom_call" | custom-call | tf_op jit(solution)/shard_map/pallas_call | solution.py:686

commit v6 on v5

--- a/solution.py
+++ b/solution.py
@@ -19,6 +19,8 @@
 GROUP = 512
 ORDER = (1, 7, 2, 6, 3, 5, 4)
 XORDER = (1, 3, 2)
+FIRST = ORDER[::-1]
+XFIRST = XORDER[::-1]
 
 
 def dot(a, b):
@@ -128,7 +130,7 @@
         load.start()
 
     pl.semaphore_wait(barrier, 2 * (NA - 1) + NX)
-    for k in ORDER:
+    for k in FIRST:
         send(tf_hbm, gt.at[a], ag1_ss.at[k], ag1_rs.at[k], on_a(k)[1])
 
     for load in loads[1:3]:
@@ -160,8 +162,10 @@
     rest = jnp.concatenate([listed, places], axis=1)
     own = g0.at[pl.ds(pl.multiple_of(a * 16, 16), 16), :]
     g0[pl.ds(pl.multiple_of(a * 16, 16), 16), :] = rest.astype(BF16)
-    for k in ORDER:
+    for k in FIRST:
         send(own, own, x_ss.at[k], x_rs.at[k], on_a(k)[1])
+
+    own_ids = jnp.broadcast_to(id_row.astype(F32), (128, SLAB)).T[:, 0:1]
 
     for load in loads[3:]:
         load.wait()
@@ -180,7 +184,7 @@
         arrived(gt.at[on_a(NA - k)[0]], ag1_rs.at[k])
 
     def widen(g, ss, rs):
-        for k in ORDER:
+        for k in FIRST:
             send(g.at[0, b], g.at[0, b], ss.at[8 + k], rs.at[8 + k], on_b(k)[1])
 
     loads[0].wait()
@@ -256,7 +260,7 @@
         + jnp.where(where_row == lane + 64, found, F32(0.0)),
         axis=0, keepdims=True,
     )
-    own_ids = jnp.broadcast_to(id_row.astype(F32), (128, SLAB)).T[:, 0:1]
+
 
     negatives, positives = [], []
     for i in range(4):
@@ -285,7 +289,7 @@
     arrived(stat_core, st_rs.at[0])
     mine = mine + stat_core[...]
     stat_a[a] = mine
-    for k in ORDER:
+    for k in FIRST:
         send(stat_a.at[a], stat_a.at[a], st_ss.at[k], st_rs.at[k], on_a(k)[1])
 
     for part, half in enumerate((negs_half, poss_half)):
@@ -303,7 +307,7 @@
                     q_own[part, rows, :] + q_core[part, rows, :].astype(F32)
                 ).astype(BF16)
 
-        for k in ORDER:
+        for k in FIRST:
             there, device = on_b(k)
             send(qb_send.at[there, h], qb_recv.at[b, h],
                  q_ss.at[8 + 8 * h + k], q_rs.at[8 + 8 * h + k], device)
@@ -312,7 +316,7 @@
     for k in ORDER:
         arrived(stat_a.at[on_a(NA - k)[0]], st_rs.at[k])
     stat_b[b] = jnp.sum(stat_a[...], axis=0)
-    for k in ORDER:
+    for k in FIRST:
         send(stat_b.at[b], stat_b.at[b], st_ss.at[8 + k], st_rs.at[8 + k], on_b(k)[1])
 
     pick = jnp.where(
@@ -361,7 +365,7 @@
             sums[0] * as_column(by_total, h)
             - (sums[1] * as_column(by_positive, h)) * as_column(share_negative, h)
         ).astype(BF16)
-        for k in ORDER:
+        for k in FIRST:
             send(qa_recv.at[h, a], qa_recv.at[h, a],
                  q_ss.at[24 + 8 * h + k], q_rs.at[24 + 8 * h + k], on_a(k)[1])
 
@@ -379,7 +383,7 @@
         rows = pl.ds(pl.multiple_of(i * 64, 64), 64)
         k_send[i] = dot(weights[rows, :], query_half[...]).astype(BF16)
 
-    for k in XORDER:
+    for k in XFIRST:
         there, device = on_x(k)
         send(k_send.at[there], k_recv.at[x], k_ss.at[k], k_rs.at[k], device)
     k_recv[x] = k_send[x]
@@ -397,7 +401,7 @@
         (key_sum - unit * jnp.sum(unit * key_sum, axis=1, keepdims=True))
         * (1.0 / key_len[quarter, 0:1])
     ).astype(BF16)
-    for k in XORDER:
+    for k in XFIRST:
         send(krg.at[x], krg.at[x], k_ss.at[4 + k], k_rs.at[4 + k], on_x(k)[1])
 
     for h in range(2):
@@ -412,7 +416,7 @@
             (query_sum - unit * jnp.sum(unit * query_sum, axis=1, keepdims=True))
             * (1.0 / len_all[rows, 0:1])
         ).astype(BF16)
-        for k in ORDER:
+        for k in FIRST:
             send(g2.at[0, b, h], g2.at[0, b, h],
                  ag2_ss.at[8 * h + k], ag2_rs.at[8 * h + k], on_b(k)[1])
         send(g2.at[0, b, h], g2.at[1, b, h], ag2_ss.at[16 + 8 * h], ag2_rs.at[16 + 8 * h], partner)
@@ -457,7 +461,7 @@
     for i in range(NA):
         rows = slice(i * 64, i * 64 + 64)
         sb_send[i] = (s_own[rows, :] + s_core[rows, :].astype(F32)).astype(BF16)
-    for k in ORDER:
+    for k in FIRST:
         there, device = on_b(k)
         send(sb_send.at[there], sb_recv.at[b], s_ss.at[8 + k], s_rs.at[8 + k], device)
     sb_recv[b] = sb_send[b]
@@ -472,7 +476,7 @@
         band = slice(i * 128, i * 128 + 128)
         p_send[band, :] = dot_rows(shifted_all[:, band], half).astype(BF16)
     for h in range(2):
-        for k in XORDER:
+        for k in XFIRST:
             there, device = on_x(k)
             send(p_send.at[pl.ds(pl.multiple_of(there * 192 + h * 96, 32), 96), :],
                  p_recv.at[h, x], p_ss.at[4 * h + k], p_rs.at[4 * h + k], device)
@@ -487,20 +491,8 @@
         gain_sum = gain_sum + jnp.sum(grad * normed_all[rows, :], axis=0, keepdims=True)
         bias_sum = bias_sum + jnp.sum(grad, axis=0, keepdims=True)
     gb_recv[x] = jnp.concatenate([gain_sum, bias_sum, jnp.zeros((6, D), F32)], axis=0)
-    for k in XORDER:
+    for k in XFIRST:
         send(gb_recv.at[x], gb_recv.at[x], p_ss.at[8 + k], p_rs.at[8 + k], on_x(k)[1])
-
-    for k in ORDER:
-        arrived(sb_recv.at[on_b(NA - k)[0]], s_rs.at[8 + k])
-    part = sb_recv[0].astype(F32)
-    for i in range(1, NA):
-        part = part + sb_recv[i].astype(F32)
-    for i in range(NA):
-        sa_send[i] = part[i * 8:i * 8 + 8, :]
-    for k in ORDER:
-        there, device = on_a(k)
-        send(sa_send.at[there], sa_recv.at[a], s_ss.at[k], s_rs.at[k], device)
-    sa_recv[a] = sa_send[a]
 
     stores = []
 
@@ -524,11 +516,23 @@
             (p_recv[h, 0].astype(F32) + p_recv[h, 1].astype(F32)) + p_recv[h, 2].astype(F32)
         ) + p_recv[h, 3].astype(F32)
         p_out[0, x, h] = total.astype(BF16)
-        for k in XORDER:
+        for k in XFIRST:
             send(p_out.at[0, x, h], p_out.at[0, x, h],
                  p_ss.at[12 + 4 * h + k], p_rs.at[12 + 4 * h + k], on_x(k)[1])
         send(p_out.at[0, x, h], p_out.at[1, x, h], p_ss.at[20 + 4 * h], p_rs.at[20 + 4 * h], partner)
         store(0, x, h, 4 * h)
+        if h == 0:
+            for k in ORDER:
+                arrived(sb_recv.at[on_b(NA - k)[0]], s_rs.at[8 + k])
+            part = sb_recv[0].astype(F32)
+            for i in range(1, NA):
+                part = part + sb_recv[i].astype(F32)
+            for i in range(NA):
+                sa_send[i] = part[i * 8:i * 8 + 8, :]
+            for k in FIRST:
+                there, device = on_a(k)
+                send(sa_send.at[there], sa_recv.at[a], s_ss.at[k], s_rs.at[k], device)
+            sa_recv[a] = sa_send[a]
 
     for k in XORDER:
         arrived(gb_recv.at[on_x(NX - k)[0]], p_rs.at[8 + k])

time: 90.7 us -> 89.2 us (0.983)
  Pallas kernels: 89.9 us -> 88.4 us
    pallas_call x1, Pallas kernels: 87.8 us -> 86.2 us  [shards(): pl.pallas_call(kernel, out_shape=(jax.ShapeDtypeStruct((16, D), F32), jax...]
where the time goes in v6:
time: 89.2 us; the launch traced here: 89 us
  Pallas kernels  88.4 us (99%)
    pallas_call x1, Pallas kernels, shards(): pl.pallas_call(kernel, out_shape=(jax.ShapeDtypeStruct((16, D), F32), jax...  86.2 us
    pallas_call x1, Pallas kernels, shards(): pl.pallas_call(finish, out_shape=(jax.ShapeDtypeStruct((ROWS, D), F32), j...  2.12 us

profile of v6, /device:TPU:1, one launch (start us, length us, event | category | flops | bytes accessed | tf_op | source)
XLA Modules:
  0.0 89.0 jit_solution(10802653603430097652)
XLA Ops:
  0.6 86.2 %shard_map.119 = (f32[16,768]{1,0:T(8,128)}, bf16[768,768]{1,0:T(8,128)(2,1)}) custom-call(bf16[4,768]{1,0:T(4,128)(2,1)} %tf_hbm.1, f32[768]{0:T(1024)} %gain_hbm.1, f32[768]{0:T(1024)} %bias_hbm.1, bf16[768,768]{1,0:T(8,128)(2,1)} %proj_hbm.1, bf16[256,768]{1,0:T(8,128)(2,1)} %emb_hbm.1, bf16[768,768]{1,0:T(8,128)(2,1)} %adapter_hbm.1, s32[256]{0:T(256)} %ids_hbm.1, ...), custom_call_target="tpu_custom_call" | custom-call | tf_op jit(solution)/shard_map/pallas_call | solution.py:605
  86.9 2.1 %shard_map.120 = (f32[4,768]{1,0:T(4,128)}, f32[768]{0:T(1024)}, f32[768]{0:T(1024)}, bf16[768,768]{1,0:T(8,128)(2,1)}, f32[6,192]{1,0:T(8,128)}) custom-call(f32[16,768]{1,0:T(8,128)} %get-tuple-element.12.small_hbm, bf16[768,768]{1,0:T(8,128)(2,1)} %get-tuple-element.13.part_hbm), custom_call_target="tpu_custom_call" | custom-call | tf_op jit(solution)/shard_map/pallas_call | solution.py:690

commit v7 on v6

--- a/solution.py
+++ b/solution.py
@@ -534,14 +534,6 @@
                 send(sa_send.at[there], sa_recv.at[a], s_ss.at[k], s_rs.at[k], device)
             sa_recv[a] = sa_send[a]
 
-    for k in XORDER:
-        arrived(gb_recv.at[on_x(NX - k)[0]], p_rs.at[8 + k])
-    small_out[4:6, :] = jnp.sum(gb_recv[...], axis=0)[0:2]
-
-    for k in ORDER:
-        arrived(sa_recv.at[on_a(NA - k)[0]], s_rs.at[k])
-    small_out[8:16, 0:256] = jnp.sum(sa_recv[...], axis=0)
-
     for h in range(2):
         for k in XORDER:
             there = on_x(NX - k)[0]
@@ -549,6 +541,14 @@
             send(p_out.at[0, there, h], p_out.at[1, there, h],
                  p_ss.at[20 + 4 * h + k], p_rs.at[20 + 4 * h + k], partner)
             store(0, there, h, 4 * h + k)
+    for k in XORDER:
+        arrived(gb_recv.at[on_x(NX - k)[0]], p_rs.at[8 + k])
+    small_out[4:6, :] = jnp.sum(gb_recv[...], axis=0)[0:2]
+
+    for k in ORDER:
+        arrived(sa_recv.at[on_a(NA - k)[0]], s_rs.at[k])
+    small_out[8:16, 0:256] = jnp.sum(sa_recv[...], axis=0)
+
     for h in range(2):
         arrived(p_out.at[1, x, h], p_rs.at[20 + 4 * h])
         store(1, x, h, 8 + 4 * h)

time: 89.2 us -> 89.2 us (level)
  no operation moved by 1% of the time
where the time goes in v7:
time: 89.2 us; the launch traced here: 89 us
  Pallas kernels  88.4 us (99%)
    pallas_call x1, Pallas kernels, shards(): pl.pallas_call(kernel, out_shape=(jax.ShapeDtypeStruct((16, D), F32), jax...  86.2 us
    pallas_call x1, Pallas kernels, shards(): pl.pallas_call(finish, out_shape=(jax.ShapeDtypeStruct((ROWS, D), F32), j...  2.12 us

profile of v7, /device:TPU:1, one launch (start us, length us, event | category | flops | bytes accessed | tf_op | source)
XLA Modules:
  0.0 89.0 jit_solution(7357723639492086343)
XLA Ops:
  0.6 86.2 %shard_map.119 = (f32[16,768]{1,0:T(8,128)}, bf16[768,768]{1,0:T(8,128)(2,1)}) custom-call(bf16[4,768]{1,0:T(4,128)(2,1)} %tf_hbm.1, f32[768]{0:T(1024)} %gain_hbm.1, f32[768]{0:T(1024)} %bias_hbm.1, bf16[768,768]{1,0:T(8,128)(2,1)} %proj_hbm.1, bf16[256,768]{1,0:T(8,128)(2,1)} %emb_hbm.1, bf16[768,768]{1,0:T(8,128)(2,1)} %adapter_hbm.1, s32[256]{0:T(256)} %ids_hbm.1, ...), custom_call_target="tpu_custom_call" | custom-call | tf_op jit(solution)/shard_map/pallas_call | solution.py:605
  86.9 2.1 %shard_map.120 = (f32[4,768]{1,0:T(4,128)}, f32[768]{0:T(1024)}, f32[768]{0:T(1024)}, bf16[768,768]{1,0:T(8,128)(2,1)}, f32[6,192]{1,0:T(8,128)}) custom-call(f32[16,768]{1,0:T(8,128)} %get-tuple-element.12.small_hbm, bf16[768,768]{1,0:T(8,128)(2,1)} %get-tuple-element.13.part_hbm), custom_call_target="tpu_custom_call" | custom-call | tf_op jit(solution)/shard_map/pallas_call | solution.py:690
